TPU v7x, 512 devices: a whole 4x4x16 slice. The times are simulated.
512 devices in a mesh: leaf: 128 (over y, z, core), rhs: 4 (over x).
Axes of the slice: x: 4, y: 4, z: 16, core: 2. Of those that a mesh axis runs over, the one named last changes fastest.
Arguments:
- coeffs: bfloat16 [64, 32768], P('rhs', 'leaf'), may hold values from -6 to 6
- near_blocks: bfloat16 [5120, 128, 128], P('leaf'), may hold values from -0.125 to 0.125
- near_scale: int32 [5120], P('leaf'), may hold values from -1 to 1
- near_target: int32 [5120], replicated, may hold values from 0 to 255, as said below
- near_source: int32 [5120], replicated, may hold values from 0 to 255, as said below
- src_basis: bfloat16 [256, 32, 128], P('leaf'), may hold values from -0.5 to 0.5
- tgt_basis: bfloat16 [256, 32, 128], P('leaf'), may hold values from -1 to 1
- couplings: bfloat16 [4096, 32, 32], P(('leaf', 'rhs')), may hold values from -0.25 to 0.25
- far_target: int32 [4096], replicated, may hold values from 0 to 255, as said below
- far_source: int32 [4096], replicated, may hold values from 0 to 255, as said below
Outputs:
- potentials: float32 [64, 32768], P('rhs', 'leaf')
Inputs may be any that keep to these rules, and one draw needn't show every extreme that they name: `near_source`: block b is held by leaf device b // 40; cluster c lies on leaf device c // 2. Of one holder's blocks at most 2 have their source cluster on one leaf device, and for every holder some leaf device supplies exactly 2. `near_target`: of one holder's blocks at most 2 have their target cluster on one leaf device, and for every holder some leaf device receives exactly 2. (Blocks are dealt to holders for load balance, independently of their block rows.). `far_source`: pair q's source cluster lies on leaf device q // 32. `far_target`: of the pairs whose sources lie on one leaf device, at most 2 have their target cluster on one leaf device, and for every such device some leaf device receives exactly 2.
All inputs are finite; a program needn't handle non-finite values.
Results may differ from a plain program's by a relative error of at most 0.0026.
Values may be sent and summed in bfloat16 or wider, within the bound.
A program may use at most 64 MiB of HBM per device.

v0:
```python
import jax
import jax.numpy as jnp
from jax import lax
from jax.sharding import PartitionSpec as P


def ranks_of(devices):
    count = devices.shape[1]
    same = devices[:, :, None] == devices[:, None, :]
    earlier = jnp.arange(count)[None, :] < jnp.arange(count)[:, None]
    return jnp.sum(same & earlier[None], axis=2, dtype=jnp.int32)


def own_row(table, index):
    return lax.dynamic_index_in_dim(table, index, 0, keepdims=False)


def slot_owners(dest, ranks, mask, cap, groups, local, empty):
    owners = lax.broadcasted_iota(jnp.int32, dest.shape, 0)
    where_to = jnp.where(mask, owners * cap + ranks, groups * cap)
    table = jnp.full((groups * cap,), empty, jnp.int32)
    return table.at[where_to.reshape(-1)].set(local.reshape(-1), mode="drop")


def collect(table, received, clusters_dev):
    selector = (table[None, :] == jnp.arange(clusters_dev, dtype=jnp.int32)[:, None]).astype(
        jnp.float32
    )
    flat = received.reshape(received.shape[0], -1)
    return jnp.dot(
        selector, flat, precision=lax.Precision.HIGHEST, preferred_element_type=jnp.float32
    )


def per_device(
    coeffs,
    near_blocks,
    near_scale,
    near_target,
    near_source,
    src_basis,
    tgt_basis,
    couplings,
    far_target,
    far_source,
):
    groups = lax.axis_size("leaf")
    mine = lax.axis_index("leaf")
    columns = coeffs.shape[0]
    clusters_dev = src_basis.shape[0]
    width = src_basis.shape[2]
    rank = src_basis.shape[1]
    blocks_dev = near_blocks.shape[0]
    cap = max(2, -(-blocks_dev // groups))
    local_x = coeffs.reshape(columns, clusters_dev, width).transpose(1, 0, 2)
    src_dev = (near_source // clusters_dev).reshape(groups, blocks_dev)
    tgt_dev = (near_target // clusters_dev).reshape(groups, blocks_dev)
    src_local = (near_source % clusters_dev).reshape(groups, blocks_dev)
    tgt_local = (near_target % clusters_dev).reshape(groups, blocks_dev)
    src_rank = ranks_of(src_dev)
    tgt_rank = ranks_of(tgt_dev)
    send_table = slot_owners(
        src_dev, src_rank, src_dev == mine, cap, groups, src_local, clusters_dev
    )
    padded_x = jnp.concatenate([local_x, jnp.zeros((1, columns, width), local_x.dtype)], axis=0)
    arrived = lax.all_to_all(padded_x[send_table], "leaf", split_axis=0, concat_axis=0, tiled=True)
    my_slots = own_row(src_dev, mine) * cap + own_row(src_rank, mine)
    sources = arrived[my_slots]
    products = jnp.einsum("bfj,bij->bfi", sources, near_blocks, preferred_element_type=jnp.float32)
    products = products * jnp.exp2(near_scale.astype(jnp.float32))[:, None, None]
    back_slots = own_row(tgt_dev, mine) * cap + own_row(tgt_rank, mine)
    back_table = (
        jnp.full((groups * cap,), blocks_dev, jnp.int32)
        .at[back_slots]
        .set(jnp.arange(blocks_dev, dtype=jnp.int32))
    )
    padded_p = jnp.concatenate([products, jnp.zeros((1, columns, width), jnp.float32)], axis=0)
    returned = lax.all_to_all(padded_p[back_table], "leaf", split_axis=0, concat_axis=0, tiled=True)
    near_table = slot_owners(
        tgt_dev, tgt_rank, tgt_dev == mine, cap, groups, tgt_local, clusters_dev
    )
    near_sum = collect(near_table, returned, clusters_dev).reshape(clusters_dev, columns, width)
    basis_x = jnp.einsum(
        "cfp,crp->cfr", local_x, src_basis, preferred_element_type=jnp.float32
    ).astype(jnp.bfloat16)
    far_leaf = far_target.shape[0] // groups
    fcap = max(2, -(-far_leaf // groups))
    ftgt_dev = (far_target // clusters_dev).reshape(groups, far_leaf)
    ftgt_local = (far_target % clusters_dev).reshape(groups, far_leaf)
    fsrc_local = (far_source % clusters_dev).reshape(groups, far_leaf)
    frank = ranks_of(ftgt_dev)
    share = lax.axis_index("rhs")
    per_share = couplings.shape[0]
    all_columns = lax.all_gather(basis_x, "rhs", axis=1, tiled=True)
    first = share * per_share
    pair_src = lax.dynamic_slice_in_dim(own_row(fsrc_local, mine), first, per_share)
    pair_dev = lax.dynamic_slice_in_dim(own_row(ftgt_dev, mine), first, per_share)
    pair_rank = lax.dynamic_slice_in_dim(own_row(frank, mine), first, per_share)
    terms = jnp.einsum(
        "qfi,qoi->qfo", all_columns[pair_src], couplings, preferred_element_type=jnp.float32
    )
    out_table = (
        jnp.full((groups * fcap,), per_share, jnp.int32)
        .at[pair_dev * fcap + pair_rank]
        .set(jnp.arange(per_share, dtype=jnp.int32))
    )
    all_cols = all_columns.shape[1]
    padded_t = jnp.concatenate([terms, jnp.zeros((1, all_cols, rank), jnp.float32)], axis=0)
    incoming = lax.all_to_all(
        padded_t[out_table].reshape(groups * fcap, all_cols * rank),
        "leaf",
        split_axis=0,
        concat_axis=0,
        tiled=True,
    )
    share_of = jnp.arange(far_leaf, dtype=jnp.int32)[None, :] // per_share
    far_table = slot_owners(
        ftgt_dev,
        frank,
        (ftgt_dev == mine) & (share_of == share),
        fcap,
        groups,
        ftgt_local,
        clusters_dev,
    )
    partial_hat = collect(far_table, incoming, clusters_dev).reshape(clusters_dev, all_cols, rank)
    far_hat = lax.psum_scatter(partial_hat, "rhs", scatter_dimension=1, tiled=True)
    far_rounded = far_hat.astype(jnp.bfloat16)
    far_sum = jnp.einsum("cfr,crp->cfp", far_rounded, tgt_basis, preferred_element_type=jnp.float32)
    total = near_sum + far_sum
    return total.transpose(1, 0, 2).reshape(columns, clusters_dev * width)


def solution(mesh):
    placed = (
        P("rhs", "leaf"),
        P("leaf", None, None),
        P("leaf"),
        P(),
        P(),
        P("leaf", None, None),
        P("leaf", None, None),
        P(("leaf", "rhs"), None, None),
        P(),
        P(),
    )
    return jax.shard_map(
        per_device, mesh=mesh, in_specs=placed, out_specs=P("rhs", "leaf"), check_vma=False
    )
```

profile of v0, /device:TPU:6, one launch (start us, length us, event | category | flops | bytes accessed | tf_op | source)
XLA Modules:
  0.0 321.1 jit_solution(1586055245250988285)
XLA Ops:
  0.0 0.8 bitcast_bitcast_fusion.1
  4.5 19.2 %scatter_custom_fusion.1 = s32[256]{0:T(256)S(1)} fusion(s32[5120]{0:T(1024)S(1)} %get-tuple-element.10, s32[5120]{0:T(1024)S(1)} %get-tuple-element.9, s32[]{:T(128)} %constant.152.clone.1), kind=kCustom, calls=%fused_computation.99 | custom fusion | bytes 1028 | tf_op jit(solution)/shard_map/scatter | solution.py:22
  23.8 1.8 gather_fusion
  25.6 20.0 %all-to-all-start = ((bf16[256,16,128]{2,1,0:T(8,128)(2,1)}), bf16[256,16,128]{2,1,0:T(8,128)(2,1)S(1)}, u32[]{:S(2)}, u32[]{:S(2)}) async-start(bf16[256,16,128]{2,1,0:T(8,128)(2,1)} %gather_fusion), calls=%async_computation | async-start | bytes 2097152 | tf_op jit(solution)/shard_map/all_to_all | solution.py:66
  45.7 11.9 %all_gather.3 = bf16[2,64,32]{2,1,0:T(8,128)(2,1)S(1)} all-gather(bf16[2,16,32]{2,1,0:T(8,128)(2,1)S(1)} %convolution_convert_fusion), channel_id=1, replica_groups=mesh['leaf'=128,'rhs'=4] {'rhs'}, dimensions={1}, use_global_device_ids=true | all-gather | bytes 10240 | tf_op jit(solution)/shard_map/all_gather | solution.py:94
  59.9 3.0 gather_fusion.4
  62.9 6.9 %copy.70 = f32[256,64,32]{2,1,0:T(8,128)} copy(f32[256,64,32]{1,2,0:T(8,128)} %gather_fusion.4) | data formatting | bytes 4194304 | tf_op jit(solution)/shard_map/gather | solution.py:110
  69.9 8.0 %all_to_all.16 = f32[128,2,2048]{2,1,0:T(2,128)} reshape(f32[256,64,32]{2,1,0:T(8,128)} %copy.70) | data formatting | bytes 4194304 | tf_op jit(solution)/shard_map/all_to_all | solution.py:109
  77.9 23.4 %all-to-all-done = bf16[256,16,128]{2,1,0:T(8,128)(2,1)S(1)} async-done(((bf16[256,16,128]{2,1,0:T(8,128)(2,1)}), bf16[256,16,128]{2,1,0:T(8,128)(2,1)S(1)}, u32[]{:S(2)}, u32[]{:S(2)}) %all-to-all-start) | async-done | bytes 1048608 | tf_op jit(solution)/shard_map/all_to_all | solution.py:66
  101.3 7.7 %all-to-all-start.2 = ((f32[128,2,2048]{2,1,0:T(2,128)}), f32[128,2,2048]{2,1,0:T(2,128)}, u32[]{:S(2)}, u32[]{:S(2)}) async-start(f32[128,2,2048]{2,1,0:T(2,128)} %all_to_all.16), calls=%async_computation.2 | async-start | bytes 4194304 | tf_op jit(solution)/shard_map/all_to_all | solution.py:109
  111.4 2.4 gather_fusion.2
  113.8 93.6 %all-to-all-done.2 = f32[128,2,2048]{2,1,0:T(2,128)} async-done(((f32[128,2,2048]{2,1,0:T(2,128)}), f32[128,2,2048]{2,1,0:T(2,128)}, u32[]{:S(2)}, u32[]{:S(2)}) %all-to-all-start.2) | async-done | bytes 2097184 | tf_op jit(solution)/shard_map/all_to_all | solution.py:109
  207.4 9.0 %all-to-all-start.1 = ((f32[256,16,128]{2,1,0:T(8,128)}), f32[256,16,128]{2,1,0:T(8,128)S(1)}, u32[]{:S(2)}, u32[]{:S(2)}) async-start(f32[256,16,128]{2,1,0:T(8,128)} %gather_fusion.2), calls=%async_computation.1 | async-start | bytes 4194304 | tf_op jit(solution)/shard_map/all_to_all | solution.py:78
  216.7 1.3 dynamic-slice.3
  218.7 15.5 %scatter_custom_fusion.3 = s32[256]{0:T(256)S(1)} fusion(s32[4096]{0:T(1024)S(1)} %get-tuple-element.12, s32[4096]{0:T(1024)S(1)} %get-tuple-element.11, s32[]{:T(128)} %constant.152.clone.1), kind=kCustom, calls=%fused_computation.97 | custom fusion | bytes 1028 | tf_op jit(solution)/shard_map/scatter | solution.py:22
  234.2 19.2 %scatter_custom_fusion = s32[256]{0:T(256)S(1)} fusion(s32[5120]{0:T(1024)S(1)} %get-tuple-element.17, s32[5120]{0:T(1024)S(1)} %get-tuple-element.18, s32[]{:T(128)} %constant.152.clone.1), kind=kCustom, calls=%fused_computation.101 | custom fusion | bytes 1028 | tf_op jit(solution)/shard_map/scatter | solution.py:22
  253.5 3.7 %all_to_all.18 = f32[256,2048]{1,0:T(8,128)} reshape(f32[128,2,2048]{2,1,0:T(2,128)} %all-to-all-done.2) | data formatting | bytes 4194304 | tf_op jit(solution)/shard_map/all_to_all | solution.py:109
  257.1 2.9 copy.71
  260.0 3.7 %fusion.9 = f32[2,64,32]{2,0,1:T(2,128)S(1)} fusion(f32[64,32,256]{2,1,0:T(8,128)} %bitcast.66, s32[256]{0:T(256)S(1)} %scatter_custom_fusion.3), kind=kOutput, calls=%fused_computation.66 | convolution fusion | flops 12583424 | bytes 2114560 | tf_op jit(solution)/shard_map/dot_general | solution.py:30
  263.8 14.5 %all-reduce.3 = bf16[2,64,32]{2,0,1:T(2,128)(2,1)S(1)} all-reduce(f32[2,64,32]{2,0,1:T(2,128)S(1)} %fusion.9), channel_id=2, replica_groups=mesh['leaf'=128,'rhs'=4] {'rhs'}, use_global_device_ids=true, to_apply=%region_8.9.clone | all-reduce | flops 4096 | bytes 24576
  278.4 36.8 %all-to-all-done.1 = f32[256,16,128]{2,1,0:T(8,128)S(1)} async-done(((f32[256,16,128]{2,1,0:T(8,128)}), f32[256,16,128]{2,1,0:T(8,128)S(1)}, u32[]{:S(2)}, u32[]{:S(2)}) %all-to-all-start.1) | async-done | bytes 2097184 | tf_op jit(solution)/shard_map/all_to_all | solution.py:78
  315.3 2.2 copy.88
  317.5 1.9 copy.64
  319.4 1.0 convolution_add_fusion
  (76 shorter events, 9.4 us)
Async XLA Ops:
  0.0 110.6 %copy-start = (bf16[40,128,128]{2,1,0:T(8,128)(2,1)S(1)}, bf16[40,128,128]{2,1,0:T(8,128)(2,1)}, u32[]{:S(2)}) copy-start(bf16[40,128,128]{2,1,0:T(8,128)(2,1)} %param.11) | copy-start | bytes 3932164
  23.7 21.9 %copy-start.3 = (bf16[16,256]{1,0:T(8,128)(2,1)S(1)}, bf16[16,256]{1,0:T(8,128)(2,1)}, u32[]{:S(2)}) copy-start(bf16[16,256]{1,0:T(8,128)(2,1)} %param.10) | copy-start | bytes 24580
  23.8 21.9 %copy-start.4 = (bf16[2,32,128]{2,1,0:T(8,128)(2,1)S(1)}, bf16[2,32,128]{2,1,0:T(8,128)(2,1)}, u32[]{:S(2)}) copy-start(bf16[2,32,128]{2,1,0:T(8,128)(2,1)} %param.15) | copy-start | bytes 49156
  23.8 34.0 %copy-start.1 = (s32[4096]{0:T(1024)S(1)}, s32[4096]{0:T(1024)}, u32[]{:S(2)}) copy-start(s32[4096]{0:T(1024)} %param.18) | copy-start | bytes 49156
  23.8 34.1 %copy-start.5 = (s32[4096]{0:T(1024)S(1)}, s32[4096]{0:T(1024)}, u32[]{:S(2)}) copy-start(s32[4096]{0:T(1024)} %param.19) | copy-start | bytes 49156
  23.8 35.9 %copy-start.2 = (bf16[8,32,32]{2,1,0:T(8,128)(2,1)S(1)}, bf16[8,32,32]{2,1,0:T(8,128)(2,1)}, u32[]{:S(2)}) copy-start(bf16[8,32,32]{2,1,0:T(8,128)(2,1)} %param.17) | copy-start | bytes 49156
  25.6 75.6 %all-to-all-start = ((bf16[256,16,128]{2,1,0:T(8,128)(2,1)}), bf16[256,16,128]{2,1,0:T(8,128)(2,1)S(1)}, u32[]{:S(2)}, u32[]{:S(2)}) async-start(bf16[256,16,128]{2,1,0:T(8,128)(2,1)} %gather_fusion), calls=%async_computation | async-start | bytes 2097152 | tf_op jit(solution)/shard_map/all_to_all | solution.py:66
  77.9 32.1 %copy-start.7 = (s32[40]{0:T(128)S(1)}, s32[40]{0:T(128)}, u32[]{:S(2)}) copy-start(s32[40]{0:T(128)} %param.12) | copy-start | bytes 484
  101.3 106.1 %all-to-all-start.2 = ((f32[128,2,2048]{2,1,0:T(2,128)}), f32[128,2,2048]{2,1,0:T(2,128)}, u32[]{:S(2)}, u32[]{:S(2)}) async-start(f32[128,2,2048]{2,1,0:T(2,128)} %all_to_all.16), calls=%async_computation.2 | async-start | bytes 4194304 | tf_op jit(solution)/shard_map/all_to_all | solution.py:109
  207.4 107.9 %all-to-all-start.1 = ((f32[256,16,128]{2,1,0:T(8,128)}), f32[256,16,128]{2,1,0:T(8,128)S(1)}, u32[]{:S(2)}, u32[]{:S(2)}) async-start(f32[256,16,128]{2,1,0:T(8,128)} %gather_fusion.2), calls=%async_computation.1 | async-start | bytes 4194304 | tf_op jit(solution)/shard_map/all_to_all | solution.py:78
  260.0 18.3 %copy-start.6 = (bf16[2,32,128]{2,1,0:T(8,128)(2,1)S(1)}, bf16[2,32,128]{2,1,0:T(8,128)(2,1)}, u32[]{:S(2)}) copy-start(bf16[2,32,128]{2,1,0:T(8,128)(2,1)} %param.16) | copy-start | bytes 49156
where the time goes:
time: 323 us; the launch traced here: 321 us
  waiting for transfers between devices  154 us (48%)
  local copies, waits for them, and re-layouts  93.4 us (29%)
  starting transfers between devices  36.7 us (11%)
  blocking collectives  26.4 us (8%)
  matrix products  5.94 us (2%)
  other arithmetic  3.76 us (1%)
    all_to_all x1, waiting for transfers between devices, per_device(): lax.all_to_all(padded_t[out_table].reshape(groups * fcap, all_cols * rank...  93.6 us
    scatter x3, local copies, waits for them, and re-layouts, slot_owners(): return table.at[where_to.reshape(-1)].set(local.reshape(-1), mode='drop')  54 us
    all_to_all x1, waiting for transfers between devices, per_device(): lax.all_to_all(padded_p[back_table], 'leaf', split_axis=0, concat_axis=0,...  36.8 us
    all_to_all x1, waiting for transfers between devices, per_device(): lax.all_to_all(padded_x[send_table], 'leaf', split_axis=0, concat_axis=0,...  23.4 us
    all_to_all x1, starting transfers between devices, per_device(): lax.all_to_all(padded_x[send_table], 'leaf', split_axis=0, concat_axis=0,...  20 us
    all_to_all x3, local copies, waits for them, and re-layouts, per_device(): lax.all_to_all(padded_t[out_table].reshape(groups * fcap, all_cols * rank...  14.6 us
    unnamed x1, blocking collectives  14.5 us
    all_gather x1, blocking collectives, per_device(): all_columns = lax.all_gather(basis_x, 'rhs', axis=1, tiled=True)  11.9 us
  transfers between devices with their start and end apart: 3, of which 3 were waited for; matrix products, arithmetic and copies ran while one was open for 19% of the time, Pallas kernels for 0%

commit v1 on v0

v1 whole, which is shorter than its diff:
```python
import jax
import jax.numpy as jnp
from jax import lax
from jax.experimental import pallas as pl
from jax.experimental.pallas import tpu as pltpu
from jax.sharding import PartitionSpec as P

MESH = pl.DeviceIdType.MESH
NY, NZ, NX = 4, 16, 4
MID = 8
BLK = 40
CHUNK = 8
NCHUNK = BLK // CHUNK
PAIRS = 32
SHARE = 8
GROUPS = ((4, 9), (0, 4), (13, 3))
Z_ORDER = (8, 7, 9, 6, 10, 5, 11, 4, 12, 3, 13, 2, 14, 1, 15)
F32, BF16 = jnp.float32, jnp.bfloat16
NT = (((1,), (1,)), ((), ()))


def kernel(
    coeffs, blocks, scale, ntgt, nsrc, src_basis, tgt_basis, couplings, ftgt, fsrc,
    out,
    x_in, blk, scale_s, ntgt_v, nsrc_s, sb, tb, coup, ftgt_v, fsrc_s,
    xg, pg, fg, bx, t2n, t2f, v2, kr, kf, acc, fa, zs_buf, zr_buf,
    lsem, zsem, ysem, csem, fsem, psem, rsem,
):
    me = lax.axis_index("leaf")
    x = lax.axis_index("rhs")
    y, z, c = me // 32, (me // 2) % 16, me % 2

    def leaf(yo, zo, co):
        return (((y + yo) % NY) * NZ + (z + zo) % NZ) * 2 + (c + co) % 2

    def at(yo, zo, co):
        return {"leaf": leaf(yo, zo, co)}

    barrier = pltpu.get_barrier_semaphore()
    for zo in Z_ORDER:
        pl.semaphore_signal(barrier, inc=1, device_id=at(0, zo, 0), device_id_type=MESH)
    for yo in (2, 1, 3):
        pl.semaphore_signal(barrier, inc=1, device_id=at(yo, 0, 0), device_id_type=MESH)
    pl.semaphore_signal(barrier, inc=1, device_id=at(0, 0, 1), device_id_type=MESH)
    for xo in range(1, NX):
        pl.semaphore_signal(barrier, inc=1, device_id={"rhs": (x + xo) % NX}, device_id_type=MESH)

    local = []
    pairs = (
        (coeffs, x_in), (src_basis, sb), (ntgt, ntgt_v), (ftgt, ftgt_v),
        (couplings, coup.at[pl.ds(x * SHARE, SHARE)]), (fsrc, fsrc_s), (nsrc, nsrc_s), (scale, scale_s),
        (blocks, blk), (tgt_basis, tb),
    )
    for i, (a, b) in enumerate(pairs):
        copy = pltpu.make_async_copy(a, b, lsem.at[i])
        copy.start()
        local.append(copy)

    started = []

    def send(src, dst, sems, index, device):
        copy = pltpu.make_async_remote_copy(
            src_ref=src, dst_ref=dst, send_sem=sems.at[0, index], recv_sem=sems.at[1, index],
            device_id=device, device_id_type=MESH,
        )
        copy.start()
        started.append(copy)
        return copy

    own = 2 * MID
    local[0].wait()
    xg[own] = x_in[:, 0:128]
    xg[own + 1] = x_in[:, 128:256]
    local[1].wait()
    for k in range(2):
        part = lax.dot_general(xg[own + k], sb[k], NT, preferred_element_type=F32)
        bx[k] = part.astype(BF16)

    local[2].wait()
    local[3].wait()
    lane = lax.broadcasted_iota(jnp.int32, (16, 128), 1)
    sub = lax.broadcasted_iota(jnp.int32, (16, 128), 0)
    near_rows = jnp.zeros((16, 128), jnp.int32)
    far_rows = jnp.zeros((16, 128), jnp.int32)
    for h in range(8):
        leaf_h = leaf(h // 2, 0, h % 2)
        first = leaf_h * BLK
        row, off = first // 128, first % 128
        after = jnp.minimum(row + 1, BLK - 1)
        back = (128 - off) % 128
        one = jnp.broadcast_to(ntgt_v[pl.ds(row, 1), :], (16, 128))
        two = jnp.broadcast_to(ntgt_v[pl.ds(after, 1), :], (16, 128))
        both = pltpu.roll(jnp.where(lane >= off, one, two), back, 1)
        near_rows = jnp.where(sub == h, both, near_rows)
        frow, foff = leaf_h // 4, (leaf_h % 4) * 32
        fone = jnp.broadcast_to(ftgt_v[pl.ds(frow, 1), :], (16, 128))
        far_rows = jnp.where(sub == h, pltpu.roll(fone, (128 - foff) % 128, 1), far_rows)
    near_rows = near_rows.astype(F32).astype(BF16)
    far_rows = far_rows.astype(F32).astype(BF16)

    def spread(rows, width, step, start):
        b = lax.broadcasted_iota(jnp.int32, (128, width), 0)
        l = lax.broadcasted_iota(jnp.int32, (128, width), 1)
        pick = jnp.where(b == (l // 16) * step + start, 1.0, 0.0).astype(BF16)
        f = lax.broadcasted_iota(jnp.int32, (16, width), 1) % 16
        return jnp.dot(rows, pick, preferred_element_type=F32) * 16.0 + f.astype(F32)

    t2n[...] = spread(near_rows, BLK * 16, 1, 0)
    t2f[0] = spread(far_rows, 256, 2, 0)
    t2f[1] = spread(far_rows, 256, 2, 1)
    r = lax.broadcasted_iota(jnp.int32, (512, 128), 0)
    z_dst = (z + r // 32 + (NZ - MID)) % NZ
    v2[...] = ((((y * NZ + z_dst) * 2 + c) * 2 + (r // 16) % 2) * 16 + r % 16).astype(F32)

    local[4].wait()
    pl.semaphore_wait(barrier, 22)

    tile = xg.at[pl.ds(own, 2)]
    z_copies = {}
    for zo in Z_ORDER:
        slot = (MID - zo) % NZ
        z_copies[slot] = send(tile, xg.at[pl.ds(2 * slot, 2)], zsem, slot, at(0, zo, 0))
    mine = coup.at[pl.ds(x * SHARE, SHARE)]
    c_copies = [
        send(mine, mine, csem, xo - 1, {"rhs": (x + xo) % NX}) for xo in range(1, NX)
    ]

    def build(i, carry):
        rows = pl.ds(pl.multiple_of(i * 32, 32), 32)
        want = v2[rows, :]
        for g in range(NCHUNK):
            for h in range(8):
                row = t2n[h : h + 1, g * 128 : (g + 1) * 128]
                kr[rows, (g * 8 + h) * 128 : (g * 8 + h + 1) * 128] = jnp.where(row == want, 1.0, 0.0).astype(BF16)
        for g in range(2):
            for h in range(8):
                for half in range(2):
                    row = t2f[g, h : h + 1, half * 128 : (half + 1) * 128]
                    at_lane = (h * 2 + half) * 128
                    kf[g, rows, at_lane : at_lane + 128] = jnp.where(row == want, 1.0, 0.0).astype(BF16)
        return carry

    lax.fori_loop(0, 16, build, 0)

    def x_span(yo, co, group):
        first, count = GROUPS[group]
        return xg.at[pl.ds(((yo * 2 + co) * NZ + first) * 2, count * 2)]

    y_copies = {}

    def forward(group):
        for yo in (2, 1, 3):
            there = (NY - yo) % NY
            y_copies[there, 0, group] = send(
                x_span(0, 0, group), x_span(there, 0, group), ysem, (there * 2) * 3 + group, at(yo, 0, 0)
            )
        relay(0, group)

    def relay(yo, group):
        y_copies[yo, 1, group] = send(
            x_span(yo, 0, group), x_span(yo, 1, group), ysem, (yo * 2 + 1) * 3 + group, at(0, 0, 1)
        )

    def wait_group(group):
        first, count = GROUPS[group]
        for slot in range(first, first + count):
            if slot != MID:
                z_copies[slot].wait_recv()

    wait_group(0)
    forward(0)

    for i in (5, 6, 7):
        local[i].wait()
    for copy in c_copies:
        copy.wait_recv()
    low_half = (lane // 32) % 2 == 1
    for j in range(PAIRS // 2):
        total = None
        for g in range(2):
            q = 2 * j + g
            mat = coup[q]
            none = jnp.zeros((32, 32), BF16)
            stack = [mat, mat, none, none] if g == 0 else [none, none, mat, mat]
            basis = bx[fsrc_s[me * PAIRS + q] % 2]
            part = lax.dot_general(basis, jnp.concatenate(stack, axis=0), NT, preferred_element_type=F32)
            total = part if total is None else total + part
        high = total.astype(BF16).astype(F32)
        fg[j * 16 : (j + 1) * 16, :] = jnp.where(low_half, total - high, high).astype(BF16)

    wait_group(1)
    forward(1)
    wait_group(2)
    forward(2)

    def f_span(yo, co):
        return fg.at[pl.ds((yo * 2 + co) * 256, 256)]

    f_copies = {}
    for yo in (2, 1, 3):
        there = (NY - yo) % NY
        f_copies[there, 0] = send(f_span(0, 0), f_span(there, 0), fsem, there * 2, at(yo, 0, 0))
    f_copies[0, 1] = send(f_span(0, 0), f_span(0, 1), fsem, 1, at(0, 0, 1))
    for group in range(3):
        for yo in (1, 3, 2):
            y_copies[yo, 0, group].wait_recv()
            relay(yo, group)
    for group in range(3):
        for yo in (0, 1, 3, 2):
            y_copies[yo, 1, group].wait_recv()

    def p_span(g, yo, co):
        return pg.at[pl.ds((g * 8 + yo * 2 + co) * 128, 128)]

    local[8].wait()
    p_copies = {}
    for g in range(NCHUNK):
        for i in range(CHUNK):
            b = g * CHUNK + i
            s = nsrc_s[me * BLK + b]
            s_leaf = s // 2
            yo = (s_leaf // 32 + NY - y) % NY
            zo = ((s_leaf // 2) % 16 + NZ + MID - z) % NZ
            co = (s_leaf + c) % 2
            index = ((yo * 2 + co) * NZ + zo) * 2 + s % 2
            term = lax.dot_general(xg[index], blk[b], NT, preferred_element_type=F32)
            factor = jnp.exp2(jnp.full((16, 128), scale_s[b], jnp.int32).astype(F32))
            at_row = g * 1024 + i * 16
            pg[at_row : at_row + 16, :] = (term * factor).astype(BF16)
        for yo in (2, 1, 3):
            there = (NY - yo) % NY
            p_copies[g, there, 0] = send(
                p_span(g, 0, 0), p_span(g, there, 0), psem, g * 8 + there * 2, at(yo, 0, 0)
            )
        p_copies[g, 0, 1] = send(p_span(g, 0, 0), p_span(g, 0, 1), psem, g * 8 + 1, at(0, 0, 1))

    for yo in (1, 3, 2):
        f_copies[yo, 0].wait_recv()
        f_copies[yo, 1] = send(f_span(yo, 0), f_span(yo, 1), fsem, yo * 2 + 1, at(0, 0, 1))
    for yo in range(NY):
        f_copies[yo, 1].wait_recv()
    wide = lax.broadcasted_iota(jnp.int32, (2048, 128), 1)
    terms = fg[...]
    zero = jnp.zeros_like(terms)
    fa[...] = jnp.dot(kf[0], jnp.where(wide < 64, terms, zero), preferred_element_type=F32)
    fa[...] += jnp.dot(kf[1], jnp.where(wide < 64, zero, terms), preferred_element_type=F32)
    for zs in range(NZ):
        s = fa[zs * 32 : (zs + 1) * 32, :]
        s = s + pltpu.roll(s, 64, 1)
        s = s + pltpu.roll(s, 32, 1)
        v = jnp.where((lane // 32) % 2 == 0, s[0:16], s[16:32])
        high = v.astype(BF16).astype(F32)
        buf = zr_buf if zs == MID else zs_buf
        buf[zs, 32:48, :] = jnp.where(lane < 64, high, v - high).astype(BF16)

    for g in range(NCHUNK):
        for yo in (1, 3, 2):
            p_copies[g, yo, 0].wait_recv()
            p_copies[g, yo, 1] = send(
                p_span(g, yo, 0), p_span(g, yo, 1), psem, g * 8 + yo * 2 + 1, at(0, 0, 1)
            )
        if g > 0:
            for yo in range(NY):
                p_copies[g - 1, yo, 1].wait_recv()
            part = jnp.dot(
                kr[:, (g - 1) * 1024 : g * 1024], pg[(g - 1) * 1024 : g * 1024, :], preferred_element_type=F32
            )
            acc[...] = part if g == 1 else acc[...] + part
    for yo in range(NY):
        p_copies[NCHUNK - 1, yo, 1].wait_recv()
    last = (NCHUNK - 1) * 1024
    o_copies = []
    acc[...] += jnp.dot(kr[:, last:], pg[last:, :], preferred_element_type=F32)
    for zo in Z_ORDER:
        zs = (MID + zo) % NZ
        zs_buf[zs, 0:32, :] = acc[zs * 32 : (zs + 1) * 32, :].astype(BF16)
        there = (MID - zo) % NZ
        o_copies.append(send(zs_buf.at[zs], zr_buf.at[there], rsem, there, at(0, zo, 0)))
    total = acc[MID * 32 : (MID + 1) * 32, :]
    far = zr_buf[MID, 32:48, :].astype(F32)
    local[9].wait()
    for zo in reversed(range(15)):
        o_copies[zo].wait_recv()
        there = (MID - Z_ORDER[zo]) % NZ
        total = total + zr_buf[there, 0:32, :].astype(F32)
        far = far + zr_buf[there, 32:48, :].astype(F32)
    far = (far + pltpu.roll(far, 64, 1)).astype(BF16).astype(F32)
    both = jnp.concatenate(
        [jnp.where(lane < 32, far, 0.0), jnp.where((lane >= 32) & (lane < 64), far, 0.0)], axis=0
    ).astype(BF16)
    basis = jnp.concatenate([tb[0], tb[1], jnp.zeros((64, 128), BF16)], axis=0)
    total = total + jnp.dot(both, basis, preferred_element_type=F32)
    out[:, 0:128] = total[0:16]
    out[:, 128:256] = total[16:32]
    for copy in started:
        copy.wait_send()


def per_device(
    coeffs, near_blocks, near_scale, near_target, near_source, src_basis, tgt_basis, couplings, far_target, far_source
):
    dma = pltpu.SemaphoreType.DMA
    vmem, smem = pltpu.VMEM, pltpu.SMEM
    return pl.pallas_call(
        kernel,
        out_shape=jax.ShapeDtypeStruct((16, 256), F32),
        in_specs=[pl.BlockSpec(memory_space=pl.ANY)] * 10,
        out_specs=pl.BlockSpec(memory_space=pltpu.VMEM),
        scratch_shapes=[
            vmem((16, 256), BF16),
            vmem((BLK, 128, 128), BF16),
            smem((BLK,), jnp.int32),
            vmem((40, 128), jnp.int32),
            smem((5120,), jnp.int32),
            vmem((2, 32, 128), BF16),
            vmem((2, 32, 128), BF16),
            vmem((PAIRS, 32, 32), BF16),
            vmem((32, 128), jnp.int32),
            smem((4096,), jnp.int32),
            vmem((256, 16, 128), BF16),
            vmem((NCHUNK * 1024, 128), BF16),
            vmem((2048, 128), BF16),
            vmem((2, 16, 32), BF16),
            vmem((16, BLK * 16), F32),
            vmem((2, 16, 256), F32),
            vmem((512, 128), F32),
            vmem((512, NCHUNK * 1024), BF16),
            vmem((2, 512, 2048), BF16),
            vmem((512, 128), F32),
            vmem((512, 128), F32),
            vmem((NZ, 48, 128), BF16),
            vmem((NZ, 48, 128), BF16),
            dma((10,)),
            dma((2, NZ)),
            dma((2, 24)),
            dma((2, 3)),
            dma((2, 8)),
            dma((2, NCHUNK * 8)),
            dma((2, NZ)),
        ],
        compiler_params=pltpu.CompilerParams(
            collective_id=0, has_side_effects=True, vmem_limit_bytes=40 * 1024 * 1024
        ),
        cost_estimate=pl.CostEstimate(flops=10**9, bytes_accessed=2 * 10**6, transcendentals=0),
        name="near_far_operator",
    )(
        coeffs, near_blocks, near_scale, near_target.reshape(40, 128), near_source, src_basis, tgt_basis,
        couplings, far_target.reshape(32, 128), far_source,
    )


def solution(mesh):
    placed = (
        P("rhs", "leaf"),
        P("leaf", None, None),
        P("leaf"),
        P(),
        P(),
        P("leaf", None, None),
        P("leaf", None, None),
        P(("leaf", "rhs"), None, None),
        P(),
        P(),
    )
    return jax.shard_map(
        per_device, mesh=mesh, in_specs=placed, out_specs=P("rhs", "leaf"), check_vma=False
    )
```

time: 323 us -> 66.3 us (0.21)
  waiting for transfers between devices: 154 us -> 0 us
  local copies, waits for them, and re-layouts: 93.4 us -> 8.43 us
  Pallas kernels: 0 us -> 56.9 us
  starting transfers between devices: 36.7 us -> 0 us
  blocking collectives: 26.4 us -> 0 us
  matrix products: 5.94 us -> 0 us
  other arithmetic: 3.76 us -> 0 us
    all_to_all x3 -> x0, waiting for transfers between devices: 154 us -> none  [the longest x1 93.6 us: per_device(): lax.all_to_all(padded_t[out_table].reshape(groups * fcap, all_cols * rank...]
    pallas_call x0 -> x1, Pallas kernels: none -> 56.9 us  [per_device(): pl.pallas_call(kernel, out_shape=jax.ShapeDtypeStruct((16, 256), F32), in...]
    scatter x5 -> x0, local copies, waits for them, and re-layouts: 55.3 us -> none  [the longest x3 54 us: slot_owners(): return table.at[where_to.reshape(-1)].set(local.reshape(-1), mode='drop')]
    all_to_all x3 -> x0, starting transfers between devices: 36.7 us -> none  [the longest x1 20 us: per_device(): lax.all_to_all(padded_x[send_table], 'leaf', split_axis=0, concat_axis=0,...]
    gather x6 -> x0, local copies, waits for them, and re-layouts: 15.3 us -> none  [the longest x2 9.95 us: per_device(): padded_t[out_table].reshape(groups * fcap, all_cols * rank)]
    all_to_all x3 -> x0, local copies, waits for them, and re-layouts: 14.6 us -> none  [per_device(): lax.all_to_all(padded_t[out_table].reshape(groups * fcap, all_cols * rank...]
    unnamed x1 -> x0, blocking collectives: 14.5 us -> none
    all_gather x1 -> x0, blocking collectives: 11.9 us -> none  [per_device(): all_columns = lax.all_gather(basis_x, 'rhs', axis=1, tiled=True)]
  transfers between devices with their start and end apart: 3 -> 0, of which waited for: 3 -> 0; matrix products, arithmetic and copies ran while one was open for 19% -> 0% of each run, Pallas kernels for 0% -> 0%
where the time goes in v1:
time: 66.3 us; the launch traced here: 65.3 us
  Pallas kernels  56.9 us (86%)
  local copies, waits for them, and re-layouts  8.43 us (13%)
    pallas_call x1, Pallas kernels, per_device(): pl.pallas_call(kernel, out_shape=jax.ShapeDtypeStruct((16, 256), F32), in...  56.9 us
    unnamed x21, local copies, waits for them, and re-layouts  8.43 us

profile of v1, /device:TPU:6, one launch (start us, length us, event | category | flops | bytes accessed | tf_op | source)
XLA Modules:
  0.0 65.3 jit_solution(683097831356633633)
XLA Ops:
  0.0 0.0 copy-start
  0.0 1.3 %copy-done = bf16[40,128,128]{2,1,0:T(8,128)(2,1)S(1)} copy-done((bf16[40,128,128]{2,1,0:T(8,128)(2,1)S(1)}, bf16[40,128,128]{2,1,0:T(8,128)(2,1)}, u32[]{:S(2)}) %copy-start) | copy-done | bytes 1310744
  1.3 0.0 copy-start.1
  1.3 0.8 %copy-done.1 = bf16[8,32,32]{2,1,0:T(8,128)(2,1)S(1)} copy-done((bf16[8,32,32]{2,1,0:T(8,128)(2,1)S(1)}, bf16[8,32,32]{2,1,0:T(8,128)(2,1)}, u32[]{:S(2)}) %copy-start.1) | copy-done | bytes 16408
  2.2 0.0 copy-start.2
  2.2 0.7 %copy-done.2 = s32[5120]{0:T(1024)S(1)} copy-done((s32[5120]{0:T(1024)S(1)}, s32[5120]{0:T(1024)}, u32[]{:S(2)}) %copy-start.2) | copy-done | bytes 20504
  2.9 0.0 copy-start.3
  2.9 0.7 %copy-done.3 = s32[5120]{0:T(1024)S(1)} copy-done((s32[5120]{0:T(1024)S(1)}, s32[5120]{0:T(1024)}, u32[]{:S(2)}) %copy-start.3) | copy-done | bytes 20504
  3.6 0.0 copy-start.4
  3.6 0.7 %copy-done.4 = bf16[2,32,128]{2,1,0:T(8,128)(2,1)S(1)} copy-done((bf16[2,32,128]{2,1,0:T(8,128)(2,1)S(1)}, bf16[2,32,128]{2,1,0:T(8,128)(2,1)}, u32[]{:S(2)}) %copy-start.4) | copy-done | bytes 16408
  4.3 0.0 copy-start.5
  4.3 0.7 %copy-done.5 = bf16[2,32,128]{2,1,0:T(8,128)(2,1)S(1)} copy-done((bf16[2,32,128]{2,1,0:T(8,128)(2,1)S(1)}, bf16[2,32,128]{2,1,0:T(8,128)(2,1)}, u32[]{:S(2)}) %copy-start.5) | copy-done | bytes 16408
  5.0 0.0 copy-start.6
  5.1 0.7 %copy-done.6 = s32[4096]{0:T(1024)S(1)} copy-done((s32[4096]{0:T(1024)S(1)}, s32[4096]{0:T(1024)}, u32[]{:S(2)}) %copy-start.6) | copy-done | bytes 16408
  5.8 0.0 copy-start.7
  5.8 0.7 %copy-done.7 = s32[4096]{0:T(1024)S(1)} copy-done((s32[4096]{0:T(1024)S(1)}, s32[4096]{0:T(1024)}, u32[]{:S(2)}) %copy-start.7) | copy-done | bytes 16408
  6.5 0.0 copy-start.8
  6.5 0.7 %copy-done.8 = bf16[16,256]{1,0:T(8,128)(2,1)S(1)} copy-done((bf16[16,256]{1,0:T(8,128)(2,1)S(1)}, bf16[16,256]{1,0:T(8,128)(2,1)}, u32[]{:S(2)}) %copy-start.8) | copy-done | bytes 8216
  7.2 0.0 copy-start.9
  7.2 0.7 %copy-done.9 = s32[40]{0:T(128)S(1)} copy-done((s32[40]{0:T(128)S(1)}, s32[40]{0:T(128)}, u32[]{:S(2)}) %copy-start.9) | copy-done | bytes 184
  7.8 56.9 %near_far_operator.1 = f32[16,256]{1,0:T(8,128)S(1)} custom-call(bf16[16,256]{1,0:T(8,128)(2,1)S(1)} %copy-done.8, bf16[40,128,128]{2,1,0:T(8,128)(2,1)S(1)} %copy-done, s32[40]{0:T(128)S(1)} %copy-done.9, s32[40,128]{1,0:T(8,128)S(1)} %bitcast.2, s32[5120]{0:T(1024)S(1)} %copy-done.3, bf16[2,32,128]{2,1,0:T(8,128)(2,1)S(1)} %copy-done.4, ...), custom_call_target="tpu_custom_call" | custom-call | flops 1000000000 | bytes 2000000 | tf_op jit(solution)/shard_map/near_far_operator/pallas_call | solution.py:304
  64.7 0.6 copy.12
Async XLA Ops:
  0.0 1.3 %copy-start = (bf16[40,128,128]{2,1,0:T(8,128)(2,1)S(1)}, bf16[40,128,128]{2,1,0:T(8,128)(2,1)}, u32[]{:S(2)}) copy-start(bf16[40,128,128]{2,1,0:T(8,128)(2,1)} %blocks.1) | copy-start | bytes 3932164
  1.3 0.8 %copy-start.1 = (bf16[8,32,32]{2,1,0:T(8,128)(2,1)S(1)}, bf16[8,32,32]{2,1,0:T(8,128)(2,1)}, u32[]{:S(2)}) copy-start(bf16[8,32,32]{2,1,0:T(8,128)(2,1)} %couplings.1) | copy-start | bytes 49156
  2.2 0.7 %copy-start.2 = (s32[5120]{0:T(1024)S(1)}, s32[5120]{0:T(1024)}, u32[]{:S(2)}) copy-start(s32[5120]{0:T(1024)} %param.13) | copy-start | bytes 61444
  2.9 0.7 %copy-start.3 = (s32[5120]{0:T(1024)S(1)}, s32[5120]{0:T(1024)}, u32[]{:S(2)}) copy-start(s32[5120]{0:T(1024)} %nsrc.1) | copy-start | bytes 61444
  3.6 0.7 %copy-start.4 = (bf16[2,32,128]{2,1,0:T(8,128)(2,1)S(1)}, bf16[2,32,128]{2,1,0:T(8,128)(2,1)}, u32[]{:S(2)}) copy-start(bf16[2,32,128]{2,1,0:T(8,128)(2,1)} %src_basis.1) | copy-start | bytes 49156
  4.3 0.7 %copy-start.5 = (bf16[2,32,128]{2,1,0:T(8,128)(2,1)S(1)}, bf16[2,32,128]{2,1,0:T(8,128)(2,1)}, u32[]{:S(2)}) copy-start(bf16[2,32,128]{2,1,0:T(8,128)(2,1)} %tgt_basis.1) | copy-start | bytes 49156
  5.0 0.7 %copy-start.6 = (s32[4096]{0:T(1024)S(1)}, s32[4096]{0:T(1024)}, u32[]{:S(2)}) copy-start(s32[4096]{0:T(1024)} %param.18) | copy-start | bytes 49156
  5.8 0.7 %copy-start.7 = (s32[4096]{0:T(1024)S(1)}, s32[4096]{0:T(1024)}, u32[]{:S(2)}) copy-start(s32[4096]{0:T(1024)} %fsrc.1) | copy-start | bytes 49156
  6.5 0.7 %copy-start.8 = (bf16[16,256]{1,0:T(8,128)(2,1)S(1)}, bf16[16,256]{1,0:T(8,128)(2,1)}, u32[]{:S(2)}) copy-start(bf16[16,256]{1,0:T(8,128)(2,1)} %coeffs.1) | copy-start | bytes 24580
  7.2 0.7 %copy-start.9 = (s32[40]{0:T(128)S(1)}, s32[40]{0:T(128)}, u32[]{:S(2)}) copy-start(s32[40]{0:T(128)} %scale.1) | copy-start | bytes 484

commit v2 on v1

v2 whole, which is shorter than its diff:
```python
import jax
import jax.numpy as jnp
from jax import lax
from jax.experimental import pallas as pl
from jax.experimental.pallas import tpu as pltpu
from jax.sharding import PartitionSpec as P

MESH = pl.DeviceIdType.MESH
NY, NZ, NX = 4, 16, 4
MID = 8
NEAR = (0, 1, 15, 2, 14, 3, 13, 4, 12, 5, 11, 6, 10, 7, 9, 8)
BLK = 40
ROWS = BLK * 8
SPAN = 384
PAIRS = 32
SHARE = 8
SPLIT = 20
CLOSE = 7
Z_ORDER = (8, 7, 9, 6, 10, 5, 11, 4, 12, 3, 13, 2, 14, 1, 15)
PLACE = (0, 1, 3, 2)
RECV_NAMES = (
    "y_own", "z_close", "z_wide", "y_line1", "y_line2", "y_line3", "core", "coup", "far", "f_swap",
    "near0", "near1", "swap0", "swap1", "z_far", "z_near0", "z_near1",
)
RECV = {name: i for i, name in enumerate(RECV_NAMES)}
SEND = {name: max(0, i - 6) for i, name in enumerate(RECV_NAMES)}
F32, BF16 = jnp.float32, jnp.bfloat16
NT = (((1,), (1,)), ((), ()))


def kernel(
    coeffs, blocks, scale, ntgt, nsrc, src_basis, tgt_basis, couplings, ftgt, fsrc,
    out,
    x_in, blk, scale_s, ntgt_v, nsrc_s, sb, tb, cp_in, coup, ftgt_v, fsrc_s,
    xg, pg, fg, bx, t2n, t2f, v2, kr, kf, acc, acc_out, acc_in, fa, fown, f_out, f_in,
    zs_buf, zr_buf, fs_buf, fr_buf,
    lsem, rsem, ssem,
):
    me = lax.axis_index("leaf")
    x = lax.axis_index("rhs")
    y, z, c = me // 32, (me // 2) % 16, me % 2

    def leaf(yo, zo, co):
        return (((y + yo) % NY) * NZ + (z + zo) % NZ) * 2 + (c + co) % 2

    def at(yo, zo, co):
        return {"leaf": leaf(yo, zo, co)}

    x_copy = pltpu.make_async_copy(coeffs, x_in, lsem.at[9])
    x_copy.start()
    barrier = pltpu.get_barrier_semaphore()
    for zo in Z_ORDER:
        pl.semaphore_signal(barrier, inc=1, device_id=at(0, zo, 0), device_id_type=MESH)
    for yo in (2, 1, 3):
        pl.semaphore_signal(barrier, inc=1, device_id=at(yo, 0, 0), device_id_type=MESH)
    pl.semaphore_signal(barrier, inc=1, device_id=at(0, 0, 1), device_id_type=MESH)
    for xo in range(1, NX):
        pl.semaphore_signal(barrier, inc=1, device_id={"rhs": (x + xo) % NX}, device_id_type=MESH)

    local = []
    pairs = (
        (couplings, cp_in), (src_basis, sb), (ntgt, ntgt_v), (ftgt, ftgt_v), (fsrc, fsrc_s),
        (nsrc, nsrc_s), (scale, scale_s), (blocks, blk), (tgt_basis, tb),
    )
    for i, (a, b) in enumerate(pairs):
        copy = pltpu.make_async_copy(a, b, lsem.at[i])
        copy.start()
        local.append(copy)

    def copy_of(src, dst, name, device):
        return pltpu.make_async_remote_copy(
            src_ref=src, dst_ref=dst, send_sem=ssem.at[SEND[name]], recv_sem=rsem.at[RECV[name]],
            device_id=device, device_id_type=MESH,
        )

    def send(src, dst, name, device):
        copy_of(src, dst, name, device).start()

    def arrived(ref, name):
        copy_of(ref, ref, name, at(0, 0, 1)).wait_recv()

    def left(ref, name):
        copy_of(ref, ref, name, at(0, 0, 1)).wait_send()

    def x_tiles(first, count):
        return xg.at[pl.ds(first, count)]

    def close_at(slot, yo):
        return (slot * NY + yo) * 2

    def wide_at(slot, yo):
        return (CLOSE * NY + yo * (NZ - CLOSE) + slot - CLOSE) * 2

    wide = (NZ - CLOSE) * 2
    x_copy.wait()
    xg[0] = x_in[:, 0:128]
    xg[1] = x_in[:, 128:256]
    pl.semaphore_wait(barrier, 22)

    own = x_tiles(0, 2)
    for yo in (2, 1, 3):
        send(own, x_tiles(close_at(0, (NY - yo) % NY), 2), "y_own", at(yo, 0, 0))
    for zo in Z_ORDER:
        slot = NEAR.index((NZ - zo) % NZ)
        if slot < CLOSE:
            send(own, x_tiles(close_at(slot, 0), 2), "z_close", at(0, zo, 0))
        else:
            send(own, x_tiles(wide_at(slot, 0), 2), "z_wide", at(0, zo, 0))

    local[0].wait()
    i32 = lax.broadcasted_iota(jnp.int32, (32, 128), 0)
    lane32 = lax.broadcasted_iota(jnp.int32, (32, 128), 1)
    for t in range(SHARE // 4):
        packed = None
        for u in range(4):
            place = jnp.where(lane32 == i32 + u * 32, 1.0, 0.0).astype(BF16)
            part = jnp.dot(cp_in[t * 4 + u], place, preferred_element_type=F32)
            packed = part if packed is None else packed + part
        coup[x * (SHARE // 4) + t] = packed.astype(BF16)
    mine = coup.at[pl.ds(x * (SHARE // 4), SHARE // 4)]
    for xo in range(1, NX):
        send(mine, mine, "coup", {"rhs": (x + xo) % NX})

    local[1].wait()
    for k in range(2):
        four = jnp.concatenate([sb[k]] * 4, axis=0)
        part = lax.dot_general(xg[k], four, NT, preferred_element_type=F32)
        bx[k] = part.astype(BF16)

    local[2].wait()
    local[3].wait()
    lane = lax.broadcasted_iota(jnp.int32, (16, 128), 1)
    sub = lax.broadcasted_iota(jnp.int32, (16, 128), 0)
    near_rows = jnp.zeros((16, 128), jnp.int32)
    far_rows = jnp.zeros((16, 128), jnp.int32)
    for yo in range(NY):
        leaf_h = leaf(yo, 0, 0)
        first = leaf_h * BLK
        row, off = first // 128, first % 128
        after = jnp.minimum(row + 1, BLK - 1)
        one = jnp.broadcast_to(ntgt_v[pl.ds(row, 1), :], (16, 128))
        two = jnp.broadcast_to(ntgt_v[pl.ds(after, 1), :], (16, 128))
        both = pltpu.roll(jnp.where(lane >= off, one, two), (128 - off) % 128, 1)
        near_rows = jnp.where(sub == PLACE[yo], both, near_rows)
        frow, foff = leaf_h // 4, (leaf_h % 4) * 32
        fone = jnp.broadcast_to(ftgt_v[pl.ds(frow, 1), :], (16, 128))
        far_rows = jnp.where(sub == PLACE[yo], pltpu.roll(fone, (128 - foff) % 128, 1), far_rows)
    near_rows = near_rows.astype(F32).astype(BF16)
    far_rows = far_rows.astype(F32).astype(BF16)

    def spread(rows, width, step, start):
        b = lax.broadcasted_iota(jnp.int32, (128, width), 0)
        l = lax.broadcasted_iota(jnp.int32, (128, width), 1)
        pick = jnp.where(b == (l // 8) * step + start, 1.0, 0.0).astype(BF16)
        f = lax.broadcasted_iota(jnp.int32, (16, width), 1) % 8
        return jnp.dot(rows, pick, preferred_element_type=F32) * 8.0 + f.astype(F32)

    t2n[...] = spread(near_rows, SPAN, 1, 0)
    t2f[0] = spread(far_rows, 128, 2, 0)
    t2f[1] = spread(far_rows, 128, 2, 1)
    r = lax.broadcasted_iota(jnp.int32, (512, 128), 0)
    z_dst = (z + (r // 16) % 16 + (NZ - MID)) % NZ
    wanted = ((y * NZ + z_dst) * 2 + (c + r // 256) % 2) * 2 + (r // 8) % 2
    v2[...] = (wanted * 8 + r % 8).astype(F32)

    def build(i, carry):
        rows = pl.ds(pl.multiple_of(i * 32, 32), 32)
        want = v2[rows, :]
        for h in range(NY):
            for g in range(SPAN // 128):
                row = t2n[h : h + 1, g * 128 : (g + 1) * 128]
                to = h * SPAN + g * 128
                kr[rows, to : to + 128] = jnp.where(row == want, 1.0, 0.0).astype(BF16)
            for g in range(2):
                row = t2f[g, h : h + 1, :]
                kf[g, rows, h * 128 : (h + 1) * 128] = jnp.where(row == want, 1.0, 0.0).astype(BF16)
        return carry

    lax.fori_loop(0, 16, build, 0)
    for u in range(2):
        for h in range(NY):
            pg[u, h * SPAN + ROWS : (h + 1) * SPAN, :] = jnp.zeros((SPAN - ROWS, 128), BF16)

    arrived(x_tiles(2, 6), "y_own")
    for zo in (3, 13, 2, 14, 1, 15):
        slot = NEAR.index((NZ - zo) % NZ)
        send(x_tiles(2, 6), x_tiles(close_at(slot, 1), 6), "z_close", at(0, zo, 0))

    for i in (4, 5, 6):
        local[i].wait()
    arrived(coup.at[pl.ds(0, 6)], "coup")
    low_half = (lane // 32) % 2 == 1
    none = jnp.zeros((32, 128), BF16)
    for j in range(0, PAIRS // 2, 2):
        two = []
        for jj in (j, j + 1):
            total = None
            for g in range(2):
                q = 2 * jj + g
                mat = coup[q // 4]
                stack = [mat, mat, none, none] if g == 0 else [none, none, mat, mat]
                basis = bx[fsrc_s[me * PAIRS + q] % 2]
                basis = jnp.where(lane // 32 == q % 4, basis, jnp.zeros_like(basis))
                part = lax.dot_general(basis, jnp.concatenate(stack, axis=0), NT, preferred_element_type=F32)
                total = part if total is None else total + part
            high = total.astype(BF16).astype(F32)
            two.append(jnp.where(low_half, total - high, high))
        for u in range(2):
            half = jnp.concatenate([t[u * 8 : (u + 1) * 8] for t in two], axis=0)
            fg[j * 8 : (j + 2) * 8, u * 128 : (u + 1) * 128] = half.astype(BF16)

    for yo in (2, 1, 3):
        there = PLACE[(NY - yo) % NY]
        send(fg.at[pl.ds(0, 128)], fg.at[pl.ds(there * 128, 128)], "far", at(yo, 0, 0))

    line = x_tiles(wide_at(CLOSE, 0), wide)
    arrived(line, "z_wide")
    for yo in (2, 1, 3):
        there = (NY - yo) % NY
        send(line, x_tiles(wide_at(CLOSE, there), wide), "y_line%d" % there, at(yo, 0, 0))
    send(line, x_tiles(128 + wide_at(CLOSE, 0), wide), "core", at(0, 0, 1))
    arrived(x_tiles(8, 48), "z_close")
    send(x_tiles(0, 56), x_tiles(128, 56), "core", at(0, 0, 1))

    def halves(v):
        high = v.astype(BF16).astype(F32)
        return jnp.where(lax.broadcasted_iota(jnp.int32, v.shape, 1) < 64, high, v - high).astype(BF16)

    arrived(fg.at[pl.ds(0, 384)], "far")
    first_pair = lax.broadcasted_iota(jnp.int32, (512, 256), 1) % 128 < 64
    terms = fg[...]
    zero = jnp.zeros_like(terms)
    fa[...] = jnp.dot(kf[0], jnp.where(first_pair, terms, zero), preferred_element_type=F32)
    fa[...] += jnp.dot(kf[1], jnp.where(first_pair, zero, terms), preferred_element_type=F32)
    even = (lane[0:8] // 32) % 2 == 0
    for part in (1, 0):
        for zs in range(NZ):
            columns = []
            for u in range(2):
                s = fa[part * 256 + zs * 16 : part * 256 + (zs + 1) * 16, u * 128 : (u + 1) * 128]
                s = s + pltpu.roll(s, 64, 1)
                s = s + pltpu.roll(s, 32, 1)
                columns.append(jnp.where(even, s[0:8], s[8:16]))
            v = jnp.concatenate(columns, axis=0)
            if part == 1:
                f_out[zs * 16 : (zs + 1) * 16, :] = halves(v)
            else:
                fown[zs * 16 : (zs + 1) * 16, :] = v
        if part == 1:
            send(f_out, f_in, "f_swap", at(0, 0, 1))

    for yo in (1, 3, 2):
        line = wide_at(CLOSE, yo)
        arrived(x_tiles(line, wide), "y_line%d" % yo)
        send(x_tiles(line, wide), x_tiles(128 + line, wide), "core", at(0, 0, 1))
    arrived(x_tiles(128, 128), "core")

    def products(u, first, count):
        for yo in (2, 1, 3):
            there = PLACE[(NY - yo) % NY]
            rows = pl.ds(first * 8, count * 8)
            send(pg.at[u, rows], pg.at[u, pl.ds(there * SPAN + first * 8, count * 8)], "near%d" % u, at(yo, 0, 0))

    local[7].wait()
    for b in range(0, BLK, 2):
        two = []
        for bb in (b, b + 1):
            s = nsrc_s[me * BLK + bb]
            s_leaf = s // 2
            yo = (s_leaf // 32 + NY - y) % NY
            zo = ((s_leaf // 2) % 16 + NZ - z) % NZ
            zo = jnp.where(zo == 0, 0, jnp.where(zo <= 8, 2 * zo - 1, 2 * (NZ - zo)))
            co = (s_leaf + c) % 2
            tile = jnp.where(zo < CLOSE, zo * NY + yo, CLOSE * NY + yo * (NZ - CLOSE) + zo - CLOSE)
            index = co * 128 + tile * 2 + s % 2
            term = lax.dot_general(xg[index], blk[bb], NT, preferred_element_type=F32)
            two.append(term * jnp.exp2(jnp.full((16, 128), scale_s[bb], jnp.int32).astype(F32)))
        for u in range(2):
            half = jnp.concatenate([t[u * 8 : (u + 1) * 8] for t in two], axis=0)
            pg[u, b * 8 : (b + 2) * 8, :] = half.astype(BF16)
        if b + 2 == SPLIT:
            products(0, 0, SPLIT)
    products(0, SPLIT, BLK - SPLIT)
    products(1, 0, BLK)

    def to_all_z(src, dst, name):
        for zo in Z_ORDER:
            slot, there = (MID + zo) % NZ, (MID - zo) % NZ
            send(src.at[pl.ds(slot * 16, 16)], dst.at[pl.ds(there * 16, 16)], name, at(0, zo, 0))

    def from_all_z(dst, name):
        arrived(dst.at[pl.ds(0, 240)], name)
        total = dst[0:16, :].astype(F32)
        for slot in range(1, NZ):
            total = total + dst[slot * 16 : (slot + 1) * 16, :].astype(F32)
        return total

    arrived(f_in, "f_swap")
    theirs = f_in[...].astype(F32)
    far_all = halves(fown[...] + theirs + pltpu.roll(theirs, 64, 1))
    fs_buf[...] = far_all
    fr_buf[MID * 16 : (MID + 1) * 16, :] = far_all[MID * 16 : (MID + 1) * 16, :]
    to_all_z(fs_buf, fr_buf, "z_far")

    for u in range(2):
        arrived(pg.at[u, pl.ds(0, 3 * ROWS)], "near%d" % u)
        acc_out[u] = jnp.dot(kr[256:512, :], pg[u], preferred_element_type=F32)
        send(acc_out.at[u], acc_in.at[u], "swap%d" % u, at(0, 0, 1))
        acc[u] = jnp.dot(kr[0:256, :], pg[u], preferred_element_type=F32)
        arrived(acc_in.at[u], "swap%d" % u)
        near_all = (acc[u] + acc_in[u]).astype(BF16)
        zs_buf[u] = near_all
        zr_buf[u, MID * 16 : (MID + 1) * 16, :] = near_all[MID * 16 : (MID + 1) * 16, :]
        to_all_z(zs_buf.at[u], zr_buf.at[u], "z_near%d" % u)
    left(x_tiles(0, 254), "y_own")
    left(coup.at[pl.ds(0, 6)], "coup")
    left(fg.at[pl.ds(0, 384)], "far")
    left(f_out, "f_swap")
    left(fs_buf.at[pl.ds(0, 240)], "z_far")
    for u in range(2):
        left(pg.at[u, pl.ds(0, 3 * ROWS)], "near%d" % u)
        left(acc_out.at[u], "swap%d" % u)
    left(zs_buf.at[0, pl.ds(0, 240)], "z_near0")
    local[8].wait()
    far = from_all_z(fr_buf, "z_far")
    far = (far + pltpu.roll(far, 64, 1)).astype(BF16).astype(F32)
    both = jnp.concatenate(
        [jnp.where(lane < 32, far, 0.0), jnp.where((lane >= 32) & (lane < 64), far, 0.0)], axis=0
    ).astype(BF16)
    basis = jnp.concatenate([tb[0], tb[1], jnp.zeros((64, 128), BF16)], axis=0)
    far = jnp.dot(both, basis, preferred_element_type=F32)
    for u in range(2):
        near = from_all_z(zr_buf.at[u], "z_near%d" % u)
        for k in range(2):
            out[u * 8 : (u + 1) * 8, k * 128 : (k + 1) * 128] = (
                near[k * 8 : (k + 1) * 8] + far[k * 16 + u * 8 : k * 16 + (u + 1) * 8]
            )
    left(zs_buf.at[1, pl.ds(0, 240)], "z_near1")


def per_device(
    coeffs, near_blocks, near_scale, near_target, near_source, src_basis, tgt_basis, couplings, far_target, far_source
):
    dma = pltpu.SemaphoreType.DMA
    vmem, smem = pltpu.VMEM, pltpu.SMEM
    return pl.pallas_call(
        kernel,
        out_shape=jax.ShapeDtypeStruct((16, 256), F32),
        in_specs=[pl.BlockSpec(memory_space=pl.ANY)] * 10,
        out_specs=pl.BlockSpec(memory_space=pltpu.VMEM),
        scratch_shapes=[
            vmem((16, 256), BF16),
            vmem((BLK, 128, 128), BF16),
            smem((BLK,), jnp.int32),
            vmem((40, 128), jnp.int32),
            smem((5120,), jnp.int32),
            vmem((2, 32, 128), BF16),
            vmem((2, 32, 128), BF16),
            vmem((SHARE, 32, 32), BF16),
            vmem((PAIRS // 4, 32, 128), BF16),
            vmem((32, 128), jnp.int32),
            smem((4096,), jnp.int32),
            vmem((256, 16, 128), BF16),
            vmem((2, NY * SPAN, 128), BF16),
            vmem((NY * 128, 256), BF16),
            vmem((2, 16, 128), BF16),
            vmem((16, SPAN), F32),
            vmem((2, 16, 128), F32),
            vmem((512, 128), F32),
            vmem((512, NY * SPAN), BF16),
            vmem((2, 512, 512), BF16),
            vmem((2, 256, 128), F32),
            vmem((2, 256, 128), F32),
            vmem((2, 256, 128), F32),
            vmem((512, 256), F32),
            vmem((256, 128), F32),
            vmem((256, 128), BF16),
            vmem((256, 128), BF16),
            vmem((2, 256, 128), BF16),
            vmem((2, 256, 128), BF16),
            vmem((256, 128), BF16),
            vmem((256, 128), BF16),
            dma((10,)),
            dma((len(RECV),)),
            dma((len(RECV) - 6,)),
        ],
        compiler_params=pltpu.CompilerParams(
            collective_id=0, has_side_effects=True, vmem_limit_bytes=60 * 1024 * 1024
        ),
        cost_estimate=pl.CostEstimate(flops=10**9, bytes_accessed=2 * 10**6, transcendentals=0),
        name="near_far_operator",
    )(
        coeffs, near_blocks, near_scale, near_target.reshape(40, 128), near_source, src_basis, tgt_basis,
        couplings, far_target.reshape(32, 128), far_source,
    )


def solution(mesh):
    placed = (
        P("rhs", "leaf"),
        P("leaf", None, None),
        P("leaf"),
        P(),
        P(),
        P("leaf", None, None),
        P("leaf", None, None),
        P(("leaf", "rhs"), None, None),
        P(),
        P(),
    )
    return jax.shard_map(
        per_device, mesh=mesh, in_specs=placed, out_specs=P("rhs", "leaf"), check_vma=False
    )
```

time: 66.3 us -> 51.1 us (0.77)
  Pallas kernels: 56.9 us -> 49.1 us
  local copies, waits for them, and re-layouts: 8.43 us -> 1.32 us
    pallas_call x1, Pallas kernels: 56.9 us -> 49.1 us  [per_device(): pl.pallas_call(kernel, out_shape=jax.ShapeDtypeStruct((16, 256), F32), in...]
    unnamed x21 -> x1, local copies, waits for them, and re-layouts: 8.43 us -> 1.32 us
where the time goes in v2:
time: 51.1 us; the launch traced here: 50.5 us
  Pallas kernels  49.1 us (96%)
  local copies, waits for them, and re-layouts  1.32 us (3%)
    pallas_call x1, Pallas kernels, per_device(): pl.pallas_call(kernel, out_shape=jax.ShapeDtypeStruct((16, 256), F32), in...  49.1 us
    unnamed x1, local copies, waits for them, and re-layouts  1.32 us

profile of v2, /device:TPU:6, one launch (start us, length us, event | category | flops | bytes accessed | tf_op | source)
XLA Modules:
  0.0 50.5 jit_solution(7954992409554018469)
XLA Ops:
  0.0 49.1 %near_far_operator.1 = f32[16,256]{1,0:T(8,128)} custom-call(bf16[16,256]{1,0:T(8,128)(2,1)} %coeffs.1, bf16[40,128,128]{2,1,0:T(8,128)(2,1)} %blocks.1, s32[40]{0:T(128)} %scale.1, s32[40,128]{1,0:T(8,128)} %bitcast.2, s32[5120]{0:T(1024)} %nsrc.1, bf16[2,32,128]{2,1,0:T(8,128)(2,1)} %src_basis.1, bf16[2,32,128]{2,1,0:T(8,128)(2,1)} %tgt_basis.1, ...), custom_call_target="tpu_custom_call" | custom-call | flops 1000000000 | bytes 2000000 | tf_op jit(solution)/shard_map/near_far_operator/pallas_call | solution.py:346
  49.1 1.3 %copy.12 = f32[16,256]{1,0:T(8,128)} copy(f32[16,256]{1,0:T(8,128)} %near_far_operator.1) | data formatting | bytes 32768

commit v3 on v2

--- a/solution.py
+++ b/solution.py
@@ -11,19 +11,23 @@
 NEAR = (0, 1, 15, 2, 14, 3, 13, 4, 12, 5, 11, 6, 10, 7, 9, 8)
 BLK = 40
 ROWS = BLK * 8
-SPAN = 384
 PAIRS = 32
 SHARE = 8
-SPLIT = 20
-CLOSE = 7
+SPLITS = (0, 16, 32, BLK)
+CLOSE = 8
+LINES = ((CLOSE, 13 - CLOSE), (13, 3))
 Z_ORDER = (8, 7, 9, 6, 10, 5, 11, 4, 12, 3, 13, 2, 14, 1, 15)
+TO_Z = Z_ORDER + (0,)
+FAR_AFTER = 1
+PARTS = 8
 PLACE = (0, 1, 3, 2)
 RECV_NAMES = (
-    "y_own", "z_close", "z_wide", "y_line1", "y_line2", "y_line3", "core", "coup", "far", "f_swap",
-    "near0", "near1", "swap0", "swap1", "z_far", "z_near0", "z_near1",
+    "y_own", "z_close", "z_line0", "z_line1", "y_line10", "y_line20", "y_line30", "y_line11", "y_line21", "y_line31", "core", "coup", "far", "f_swap", "pair",
+    "dense0", "dense1", "dense2", "dense3", "dense4", "dense5", "dense6", "dense7",
+    "z_far", "z_near0", "z_near1", "z_near2", "z_near3",
 )
 RECV = {name: i for i, name in enumerate(RECV_NAMES)}
-SEND = {name: max(0, i - 6) for i, name in enumerate(RECV_NAMES)}
+SEND = dict(zip(RECV_NAMES, (0, 0, 0, 0, 0, 0, 0, 0, 0, 0, 0, 1, 2, 3, 4, 5, 5, 5, 5, 5, 5, 5, 5, 6, 7, 7, 7, 7)))
 F32, BF16 = jnp.float32, jnp.bfloat16
 NT = (((1,), (1,)), ((), ()))
 
@@ -32,9 +36,9 @@
     coeffs, blocks, scale, ntgt, nsrc, src_basis, tgt_basis, couplings, ftgt, fsrc,
     out,
     x_in, blk, scale_s, ntgt_v, nsrc_s, sb, tb, cp_in, coup, ftgt_v, fsrc_s,
-    xg, pg, fg, bx, t2n, t2f, v2, kr, kf, acc, acc_out, acc_in, fa, fown, f_out, f_in,
+    xg, pp, fg, bx, t2n, t2f, kr, kf, acc, ys_buf, yr_buf, fa, fown, f_out, f_in,
     zs_buf, zr_buf, fs_buf, fr_buf,
-    lsem, rsem, ssem,
+    index_s, lsem, rsem, ssem,
 ):
     me = lax.axis_index("leaf")
     x = lax.axis_index("rhs")
@@ -91,7 +95,10 @@
     def wide_at(slot, yo):
         return (CLOSE * NY + yo * (NZ - CLOSE) + slot - CLOSE) * 2
 
-    wide = (NZ - CLOSE) * 2
+    def line_of(core, yo, group):
+        first, count = LINES[group]
+        return x_tiles(core * 128 + wide_at(first, yo), count * 2)
+
     x_copy.wait()
     xg[0] = x_in[:, 0:128]
     xg[1] = x_in[:, 128:256]
@@ -105,7 +112,7 @@
         if slot < CLOSE:
             send(own, x_tiles(close_at(slot, 0), 2), "z_close", at(0, zo, 0))
         else:
-            send(own, x_tiles(wide_at(slot, 0), 2), "z_wide", at(0, zo, 0))
+            send(own, x_tiles(wide_at(slot, 0), 2), "z_line%d" % (slot >= 13), at(0, zo, 0))
 
     local[0].wait()
     i32 = lax.broadcasted_iota(jnp.int32, (32, 128), 0)
@@ -131,17 +138,15 @@
     local[3].wait()
     lane = lax.broadcasted_iota(jnp.int32, (16, 128), 1)
     sub = lax.broadcasted_iota(jnp.int32, (16, 128), 0)
-    near_rows = jnp.zeros((16, 128), jnp.int32)
+    first = (me // 2) * 2 * BLK
+    row, off = first // 128, first % 128
+    after = jnp.minimum(row + 1, BLK - 1)
+    one = jnp.broadcast_to(ntgt_v[pl.ds(row, 1), :], (16, 128))
+    two = jnp.broadcast_to(ntgt_v[pl.ds(after, 1), :], (16, 128))
+    near_rows = pltpu.roll(jnp.where(lane >= off, one, two), (128 - off) % 128, 1)
     far_rows = jnp.zeros((16, 128), jnp.int32)
     for yo in range(NY):
         leaf_h = leaf(yo, 0, 0)
-        first = leaf_h * BLK
-        row, off = first // 128, first % 128
-        after = jnp.minimum(row + 1, BLK - 1)
-        one = jnp.broadcast_to(ntgt_v[pl.ds(row, 1), :], (16, 128))
-        two = jnp.broadcast_to(ntgt_v[pl.ds(after, 1), :], (16, 128))
-        both = pltpu.roll(jnp.where(lane >= off, one, two), (128 - off) % 128, 1)
-        near_rows = jnp.where(sub == PLACE[yo], both, near_rows)
         frow, foff = leaf_h // 4, (leaf_h % 4) * 32
         fone = jnp.broadcast_to(ftgt_v[pl.ds(frow, 1), :], (16, 128))
         far_rows = jnp.where(sub == PLACE[yo], pltpu.roll(fone, (128 - foff) % 128, 1), far_rows)
@@ -155,34 +160,42 @@
         f = lax.broadcasted_iota(jnp.int32, (16, width), 1) % 8
         return jnp.dot(rows, pick, preferred_element_type=F32) * 8.0 + f.astype(F32)
 
-    t2n[...] = spread(near_rows, SPAN, 1, 0)
+    t2n[...] = spread(near_rows, 2 * ROWS, 1, 0)
     t2f[0] = spread(far_rows, 128, 2, 0)
     t2f[1] = spread(far_rows, 128, 2, 1)
-    r = lax.broadcasted_iota(jnp.int32, (512, 128), 0)
-    z_dst = (z + (r // 16) % 16 + (NZ - MID)) % NZ
-    wanted = ((y * NZ + z_dst) * 2 + (c + r // 256) % 2) * 2 + (r // 8) % 2
-    v2[...] = (wanted * 8 + r % 8).astype(F32)
-
-    def build(i, carry):
-        rows = pl.ds(pl.multiple_of(i * 32, 32), 32)
-        want = v2[rows, :]
-        for h in range(NY):
-            for g in range(SPAN // 128):
-                row = t2n[h : h + 1, g * 128 : (g + 1) * 128]
-                to = h * SPAN + g * 128
-                kr[rows, to : to + 128] = jnp.where(row == want, 1.0, 0.0).astype(BF16)
+    in_16 = sub.astype(F32)
+
+    def ones(row, leaf_to):
+        return jnp.where(row == in_16 + leaf_to * 16.0, 1.0, 0.0).astype(BF16)
+
+    far_lanes = [[jnp.broadcast_to(t2f[g, h : h + 1, :], (16, 128)) for h in range(NY)] for g in range(2)]
+
+    def build_far(i, carry):
+        for part in range(2):
+            rows = pl.ds(pl.multiple_of(part * 256 + i * 16, 16), 16)
+            leaf_to = ((y * NZ + (z + i + NZ - MID) % NZ) * 2 + (c + part) % 2).astype(F32)
             for g in range(2):
-                row = t2f[g, h : h + 1, :]
-                kf[g, rows, h * 128 : (h + 1) * 128] = jnp.where(row == want, 1.0, 0.0).astype(BF16)
+                for h in range(NY):
+                    kf[g, rows, h * 128 : (h + 1) * 128] = ones(far_lanes[g][h], leaf_to)
         return carry
 
-    lax.fori_loop(0, 16, build, 0)
-    for u in range(2):
-        for h in range(NY):
-            pg[u, h * SPAN + ROWS : (h + 1) * SPAN, :] = jnp.zeros((SPAN - ROWS, 128), BF16)
+    near_lanes = [jnp.broadcast_to(t2n[0:1, g * 128 : (g + 1) * 128], (16, 128)) for g in range(2 * ROWS // 128)]
+
+    def build_near(i, carry):
+        p, yo = i // NY, i % NY
+        for slot in range(2):
+            zo = MID + p if slot == 0 else MID - 1 - p
+            rows = pl.ds(pl.multiple_of(i * 32 + slot * 16, 16), 16)
+            leaf_to = ((((y + yo) % NY) * NZ + (z + zo) % NZ) * 2 + c).astype(F32)
+            for g, row in enumerate(near_lanes):
+                kr[rows, g * 128 : (g + 1) * 128] = ones(row, leaf_to)
+        return carry
+
+    lax.fori_loop(0, 16, build_far, 0)
+    lax.fori_loop(0, PARTS * NY, build_near, 0)
 
     arrived(x_tiles(2, 6), "y_own")
-    for zo in (3, 13, 2, 14, 1, 15):
+    for zo in Z_ORDER[16 - CLOSE :]:
         slot = NEAR.index((NZ - zo) % NZ)
         send(x_tiles(2, 6), x_tiles(close_at(slot, 1), 6), "z_close", at(0, zo, 0))
 
@@ -213,14 +226,27 @@
         there = PLACE[(NY - yo) % NY]
         send(fg.at[pl.ds(0, 128)], fg.at[pl.ds(there * 128, 128)], "far", at(yo, 0, 0))
 
-    line = x_tiles(wide_at(CLOSE, 0), wide)
-    arrived(line, "z_wide")
-    for yo in (2, 1, 3):
-        there = (NY - yo) % NY
-        send(line, x_tiles(wide_at(CLOSE, there), wide), "y_line%d" % there, at(yo, 0, 0))
-    send(line, x_tiles(128 + wide_at(CLOSE, 0), wide), "core", at(0, 0, 1))
-    arrived(x_tiles(8, 48), "z_close")
-    send(x_tiles(0, 56), x_tiles(128, 56), "core", at(0, 0, 1))
+    def find(bb, carry):
+        s = nsrc_s[me * BLK + bb]
+        s_leaf = s // 2
+        yo = (s_leaf // 32 + NY - y) % NY
+        zo = ((s_leaf // 2) % 16 + NZ - z) % NZ
+        zo = jnp.where(zo == 0, 0, jnp.where(zo <= 8, 2 * zo - 1, 2 * (NZ - zo)))
+        co = (s_leaf + c) % 2
+        tile = jnp.where(zo < CLOSE, zo * NY + yo, CLOSE * NY + yo * (NZ - CLOSE) + zo - CLOSE)
+        index_s[bb] = co * 128 + tile * 2 + s % 2
+        return carry
+
+    lax.fori_loop(0, BLK, find, 0)
+    for group in range(2):
+        line = line_of(0, 0, group)
+        arrived(line, "z_line%d" % group)
+        for yo in (2, 1, 3):
+            there = (NY - yo) % NY
+            send(line, line_of(0, there, group), "y_line%d%d" % (there, group), at(yo, 0, 0))
+        send(line, line_of(1, 0, group), "core", at(0, 0, 1))
+    arrived(x_tiles(8, (CLOSE - 1) * 8), "z_close")
+    send(x_tiles(0, CLOSE * 8), x_tiles(128, CLOSE * 8), "core", at(0, 0, 1))
 
     def halves(v):
         high = v.astype(BF16).astype(F32)
@@ -249,93 +275,103 @@
         if part == 1:
             send(f_out, f_in, "f_swap", at(0, 0, 1))
 
-    for yo in (1, 3, 2):
-        line = wide_at(CLOSE, yo)
-        arrived(x_tiles(line, wide), "y_line%d" % yo)
-        send(x_tiles(line, wide), x_tiles(128 + line, wide), "core", at(0, 0, 1))
+    for group in range(2):
+        for yo in (1, 3, 2):
+            line = line_of(0, yo, group)
+            arrived(line, "y_line%d%d" % (yo, group))
+            send(line, line_of(1, yo, group), "core", at(0, 0, 1))
     arrived(x_tiles(128, 128), "core")
 
-    def products(u, first, count):
-        for yo in (2, 1, 3):
-            there = PLACE[(NY - yo) % NY]
-            rows = pl.ds(first * 8, count * 8)
-            send(pg.at[u, rows], pg.at[u, pl.ds(there * SPAN + first * 8, count * 8)], "near%d" % u, at(yo, 0, 0))
+    def share(first, count):
+        rows = pl.ds(pl.multiple_of(c * ROWS + first * 8, 16), count * 8)
+        send(pp.at[:, rows], pp.at[:, rows], "pair", at(0, 0, 1))
 
     local[7].wait()
     for b in range(0, BLK, 2):
         two = []
         for bb in (b, b + 1):
-            s = nsrc_s[me * BLK + bb]
-            s_leaf = s // 2
-            yo = (s_leaf // 32 + NY - y) % NY
-            zo = ((s_leaf // 2) % 16 + NZ - z) % NZ
-            zo = jnp.where(zo == 0, 0, jnp.where(zo <= 8, 2 * zo - 1, 2 * (NZ - zo)))
-            co = (s_leaf + c) % 2
-            tile = jnp.where(zo < CLOSE, zo * NY + yo, CLOSE * NY + yo * (NZ - CLOSE) + zo - CLOSE)
-            index = co * 128 + tile * 2 + s % 2
+            index = index_s[bb]
             term = lax.dot_general(xg[index], blk[bb], NT, preferred_element_type=F32)
             two.append(term * jnp.exp2(jnp.full((16, 128), scale_s[bb], jnp.int32).astype(F32)))
+        rows = pl.ds(pl.multiple_of(c * ROWS + b * 8, 16), 16)
         for u in range(2):
             half = jnp.concatenate([t[u * 8 : (u + 1) * 8] for t in two], axis=0)
-            pg[u, b * 8 : (b + 2) * 8, :] = half.astype(BF16)
-        if b + 2 == SPLIT:
-            products(0, 0, SPLIT)
-    products(0, SPLIT, BLK - SPLIT)
-    products(1, 0, BLK)
-
-    def to_all_z(src, dst, name):
-        for zo in Z_ORDER:
-            slot, there = (MID + zo) % NZ, (MID - zo) % NZ
-            send(src.at[pl.ds(slot * 16, 16)], dst.at[pl.ds(there * 16, 16)], name, at(0, zo, 0))
-
-    def from_all_z(dst, name):
-        arrived(dst.at[pl.ds(0, 240)], name)
-        total = dst[0:16, :].astype(F32)
-        for slot in range(1, NZ):
-            total = total + dst[slot * 16 : (slot + 1) * 16, :].astype(F32)
-        return total
-
-    arrived(f_in, "f_swap")
-    theirs = f_in[...].astype(F32)
-    far_all = halves(fown[...] + theirs + pltpu.roll(theirs, 64, 1))
-    fs_buf[...] = far_all
-    fr_buf[MID * 16 : (MID + 1) * 16, :] = far_all[MID * 16 : (MID + 1) * 16, :]
-    to_all_z(fs_buf, fr_buf, "z_far")
-
-    for u in range(2):
-        arrived(pg.at[u, pl.ds(0, 3 * ROWS)], "near%d" % u)
-        acc_out[u] = jnp.dot(kr[256:512, :], pg[u], preferred_element_type=F32)
-        send(acc_out.at[u], acc_in.at[u], "swap%d" % u, at(0, 0, 1))
-        acc[u] = jnp.dot(kr[0:256, :], pg[u], preferred_element_type=F32)
-        arrived(acc_in.at[u], "swap%d" % u)
-        near_all = (acc[u] + acc_in[u]).astype(BF16)
-        zs_buf[u] = near_all
-        zr_buf[u, MID * 16 : (MID + 1) * 16, :] = near_all[MID * 16 : (MID + 1) * 16, :]
-        to_all_z(zs_buf.at[u], zr_buf.at[u], "z_near%d" % u)
+            high = half.astype(BF16)
+            pp[0, rows, u * 128 : (u + 1) * 128] = high
+            pp[1, rows, u * 128 : (u + 1) * 128] = (half - high.astype(F32)).astype(BF16)
+        if b + 2 in SPLITS:
+            first = SPLITS[SPLITS.index(b + 2) - 1]
+            share(first, b + 2 - first)
+
+    arrived(pp.at[:, pl.ds(0, ROWS)], "pair")
+    for p in range(PARTS):
+        part = kr[p * 128 : (p + 1) * 128, :]
+        sums = jnp.dot(part, pp[0], preferred_element_type=F32)
+        sums = sums + jnp.dot(part, pp[1], preferred_element_type=F32)
+        acc[p] = sums[0:32]
+        for yo in range(1, NY):
+            ys_buf[p, yo] = sums[yo * 32 : (yo + 1) * 32].astype(BF16)
+        for yo in (2, 1, 3):
+            send(ys_buf.at[p, yo], yr_buf.at[p, (NY - yo) % NY], "dense%d" % p, at(yo, 0, 0))
+        if p == FAR_AFTER:
+            arrived(f_in, "f_swap")
+            theirs = f_in[...].astype(F32)
+            far_all = halves(fown[...] + theirs + pltpu.roll(theirs, 64, 1))
+            fs_buf[...] = far_all
+            fr_buf[MID * 16 : (MID + 1) * 16, :] = far_all[MID * 16 : (MID + 1) * 16, :]
+            for zo in Z_ORDER:
+                slot, there = (MID + zo) % NZ, (MID - zo) % NZ
+                send(fs_buf.at[pl.ds(slot * 16, 16)], fr_buf.at[pl.ds(there * 16, 16)], "z_far", at(0, zo, 0))
+
+
+    for p in range(PARTS):
+        arrived(yr_buf.at[p, pl.ds(1, 3)], "dense%d" % p)
+        total = acc[p]
+        for yo in range(1, NY):
+            total = total + yr_buf[p, yo].astype(F32)
+        total = total.astype(BF16)
+        zs_buf[p * 32 : (p + 1) * 32, :] = total
+        for i in range(2):
+            zo = TO_Z[p * 2 + i]
+            if zo == 0:
+                zr_buf[(p * 2 + i) * 16 : (p * 2 + i + 1) * 16, :] = total[i * 16 : (i + 1) * 16]
+            else:
+                there = TO_Z.index(NZ - zo)
+                send(
+                    zs_buf.at[pl.ds((p * 2 + i) * 16, 16)], zr_buf.at[pl.ds(there * 16, 16)],
+                    "z_near%d" % (there // 4), at(0, zo, 0),
+                )
     left(x_tiles(0, 254), "y_own")
     left(coup.at[pl.ds(0, 6)], "coup")
     left(fg.at[pl.ds(0, 384)], "far")
     left(f_out, "f_swap")
     left(fs_buf.at[pl.ds(0, 240)], "z_far")
-    for u in range(2):
-        left(pg.at[u, pl.ds(0, 3 * ROWS)], "near%d" % u)
-        left(acc_out.at[u], "swap%d" % u)
-    left(zs_buf.at[0, pl.ds(0, 240)], "z_near0")
+    left(pp.at[:, pl.ds(0, ROWS)], "pair")
+    left(ys_buf.at[:, pl.ds(1, 3)], "dense0")
     local[8].wait()
-    far = from_all_z(fr_buf, "z_far")
+    arrived(fr_buf.at[pl.ds(0, 240)], "z_far")
+    far = fr_buf[0:16, :].astype(F32)
+    for slot in range(1, NZ):
+        far = far + fr_buf[slot * 16 : (slot + 1) * 16, :].astype(F32)
     far = (far + pltpu.roll(far, 64, 1)).astype(BF16).astype(F32)
     both = jnp.concatenate(
         [jnp.where(lane < 32, far, 0.0), jnp.where((lane >= 32) & (lane < 64), far, 0.0)], axis=0
     ).astype(BF16)
     basis = jnp.concatenate([tb[0], tb[1], jnp.zeros((64, 128), BF16)], axis=0)
     far = jnp.dot(both, basis, preferred_element_type=F32)
+    near = zr_buf[240:256, :].astype(F32)
+    for p in range(4):
+        count = 4 if p < 3 else 3
+        arrived(zr_buf.at[pl.ds(p * 64, count * 16)], "z_near%d" % p)
+        for slot in range(p * 4, p * 4 + count):
+            near = near + zr_buf[slot * 16 : (slot + 1) * 16, :].astype(F32)
     for u in range(2):
-        near = from_all_z(zr_buf.at[u], "z_near%d" % u)
         for k in range(2):
             out[u * 8 : (u + 1) * 8, k * 128 : (k + 1) * 128] = (
-                near[k * 8 : (k + 1) * 8] + far[k * 16 + u * 8 : k * 16 + (u + 1) * 8]
+                near[k * 8 : (k + 1) * 8, u * 128 : (u + 1) * 128]
+                + far[k * 16 + u * 8 : k * 16 + (u + 1) * 8]
             )
-    left(zs_buf.at[1, pl.ds(0, 240)], "z_near1")
+    left(zs_buf.at[pl.ds(0, 240)], "z_near0")
 
 
 def per_device(
@@ -361,28 +397,28 @@
             vmem((32, 128), jnp.int32),
             smem((4096,), jnp.int32),
             vmem((256, 16, 128), BF16),
-            vmem((2, NY * SPAN, 128), BF16),
+            vmem((2, 2 * ROWS, 256), BF16),
             vmem((NY * 128, 256), BF16),
             vmem((2, 16, 128), BF16),
-            vmem((16, SPAN), F32),
+            vmem((16, 2 * ROWS), F32),
             vmem((2, 16, 128), F32),
-            vmem((512, 128), F32),
-            vmem((512, NY * SPAN), BF16),
+            vmem((1024, 2 * ROWS), BF16),
             vmem((2, 512, 512), BF16),
-            vmem((2, 256, 128), F32),
-            vmem((2, 256, 128), F32),
-            vmem((2, 256, 128), F32),
+            vmem((PARTS, 32, 256), F32),
+            vmem((PARTS, NY, 32, 256), BF16),
+            vmem((PARTS, NY, 32, 256), BF16),
             vmem((512, 256), F32),
             vmem((256, 128), F32),
             vmem((256, 128), BF16),
             vmem((256, 128), BF16),
-            vmem((2, 256, 128), BF16),
-            vmem((2, 256, 128), BF16),
+            vmem((256, 256), BF16),
+            vmem((256, 256), BF16),
             vmem((256, 128), BF16),
             vmem((256, 128), BF16),
+            smem((BLK,), jnp.int32),
             dma((10,)),
             dma((len(RECV),)),
-            dma((len(RECV) - 6,)),
+            dma((8,)),
         ],
         compiler_params=pltpu.CompilerParams(
             collective_id=0, has_side_effects=True, vmem_limit_bytes=60 * 1024 * 1024

time: 51.1 us -> 47.4 us (0.928)
  Pallas kernels: 49.1 us -> 45.6 us
    pallas_call x1, Pallas kernels: 49.1 us -> 45.6 us  [per_device(): pl.pallas_call(kernel, out_shape=jax.ShapeDtypeStruct((16, 256), F32), in...]
where the time goes in v3:
time: 47.4 us; the launch traced here: 47 us
  Pallas kernels  45.6 us (96%)
  local copies, waits for them, and re-layouts  1.32 us (3%)
    pallas_call x1, Pallas kernels, per_device(): pl.pallas_call(kernel, out_shape=jax.ShapeDtypeStruct((16, 256), F32), in...  45.6 us
    unnamed x1, local copies, waits for them, and re-layouts  1.32 us

profile of v3, /device:TPU:6, one launch (start us, length us, event | category | flops | bytes accessed | tf_op | source)
XLA Modules:
  0.0 47.0 jit_solution(795106259497097278)
XLA Ops:
  0.0 45.6 %near_far_operator.1 = f32[16,256]{1,0:T(8,128)} custom-call(bf16[16,256]{1,0:T(8,128)(2,1)} %coeffs.1, bf16[40,128,128]{2,1,0:T(8,128)(2,1)} %blocks.1, s32[40]{0:T(128)} %scale.1, s32[40,128]{1,0:T(8,128)} %bitcast.2, s32[5120]{0:T(1024)} %nsrc.1, bf16[2,32,128]{2,1,0:T(8,128)(2,1)} %src_basis.1, bf16[2,32,128]{2,1,0:T(8,128)(2,1)} %tgt_basis.1, ...), custom_call_target="tpu_custom_call" | custom-call | flops 1000000000 | bytes 2000000 | tf_op jit(solution)/shard_map/near_far_operator/pallas_call | solution.py:382
  45.6 1.3 %copy.12 = f32[16,256]{1,0:T(8,128)} copy(f32[16,256]{1,0:T(8,128)} %near_far_operator.1) | data formatting | bytes 32768

commit v4 on v3

--- a/solution.py
+++ b/solution.py
@@ -14,20 +14,21 @@
 PAIRS = 32
 SHARE = 8
 SPLITS = (0, 16, 32, BLK)
-CLOSE = 8
+CLOSE = 7
 LINES = ((CLOSE, 13 - CLOSE), (13, 3))
 Z_ORDER = (8, 7, 9, 6, 10, 5, 11, 4, 12, 3, 13, 2, 14, 1, 15)
 TO_Z = Z_ORDER + (0,)
 FAR_AFTER = 1
+DIRECT = (4, 12, 3, 13, 2, 14, 1, 15)
 PARTS = 8
 PLACE = (0, 1, 3, 2)
 RECV_NAMES = (
-    "y_own", "z_close", "z_line0", "z_line1", "y_line10", "y_line20", "y_line30", "y_line11", "y_line21", "y_line31", "core", "coup", "far", "f_swap", "pair",
+    "y_own", "z_own", "z_close", "z_line0", "z_line1", "y_line10", "y_line20", "y_line30", "y_line11", "y_line21", "y_line31", "core", "coup", "far", "f_swap", "pair",
     "dense0", "dense1", "dense2", "dense3", "dense4", "dense5", "dense6", "dense7",
     "z_far", "z_near0", "z_near1", "z_near2", "z_near3",
 )
 RECV = {name: i for i, name in enumerate(RECV_NAMES)}
-SEND = dict(zip(RECV_NAMES, (0, 0, 0, 0, 0, 0, 0, 0, 0, 0, 0, 1, 2, 3, 4, 5, 5, 5, 5, 5, 5, 5, 5, 6, 7, 7, 7, 7)))
+SEND = dict(zip(RECV_NAMES, (0, 0, 0, 0, 0, 0, 0, 0, 0, 0, 0, 0, 1, 2, 3, 4, 5, 5, 5, 5, 5, 5, 5, 5, 6, 7, 7, 7, 7)))
 F32, BF16 = jnp.float32, jnp.bfloat16
 NT = (((1,), (1,)), ((), ()))
 
@@ -53,7 +54,7 @@
     x_copy = pltpu.make_async_copy(coeffs, x_in, lsem.at[9])
     x_copy.start()
     barrier = pltpu.get_barrier_semaphore()
-    for zo in Z_ORDER:
+    for zo in DIRECT:
         pl.semaphore_signal(barrier, inc=1, device_id=at(0, zo, 0), device_id_type=MESH)
     for yo in (2, 1, 3):
         pl.semaphore_signal(barrier, inc=1, device_id=at(yo, 0, 0), device_id_type=MESH)
@@ -102,17 +103,17 @@
     x_copy.wait()
     xg[0] = x_in[:, 0:128]
     xg[1] = x_in[:, 128:256]
-    pl.semaphore_wait(barrier, 22)
+    pl.semaphore_wait(barrier, 15)
 
     own = x_tiles(0, 2)
     for yo in (2, 1, 3):
         send(own, x_tiles(close_at(0, (NY - yo) % NY), 2), "y_own", at(yo, 0, 0))
-    for zo in Z_ORDER:
-        slot = NEAR.index((NZ - zo) % NZ)
-        if slot < CLOSE:
-            send(own, x_tiles(close_at(slot, 0), 2), "z_close", at(0, zo, 0))
-        else:
-            send(own, x_tiles(wide_at(slot, 0), 2), "z_line%d" % (slot >= 13), at(0, zo, 0))
+    def piece(zo):
+        slot = NEAR.index(zo % NZ)
+        return x_tiles(close_at(slot, 0) if slot < CLOSE else wide_at(slot, 0), 2)
+
+    for zo in DIRECT:
+        send(own, piece(-zo), "z_own", at(0, zo, 0))
 
     local[0].wait()
     i32 = lax.broadcasted_iota(jnp.int32, (32, 128), 0)
@@ -194,11 +195,17 @@
     lax.fori_loop(0, 16, build_far, 0)
     lax.fori_loop(0, PARTS * NY, build_near, 0)
 
-    arrived(x_tiles(2, 6), "y_own")
-    for zo in Z_ORDER[16 - CLOSE :]:
-        slot = NEAR.index((NZ - zo) % NZ)
-        send(x_tiles(2, 6), x_tiles(close_at(slot, 1), 6), "z_close", at(0, zo, 0))
-
+    arrived(x_tiles(8, 16), "z_own")
+    for zo in (4, 3, 13, 2, 14, 1, 15):
+        far = zo + 4 if zo < MID else zo - 4
+        send(piece(zo), piece(far), "z_line%d" % (NEAR.index(far) >= 13), at(0, zo - far, 0))
+    def close_forward():
+        arrived(x_tiles(2, 6), "y_own")
+        for zo in Z_ORDER[16 - CLOSE :]:
+            slot = NEAR.index((NZ - zo) % NZ)
+            send(x_tiles(2, 6), x_tiles(close_at(slot, 1), 6), "z_close", at(0, zo, 0))
+
+    pl.when(c == 0)(close_forward)
     for i in (4, 5, 6):
         local[i].wait()
     arrived(coup.at[pl.ds(0, 6)], "coup")
@@ -240,12 +247,13 @@
     lax.fori_loop(0, BLK, find, 0)
     for group in range(2):
         line = line_of(0, 0, group)
-        arrived(line, "z_line%d" % group)
+        arrived(x_tiles(wide_at(13, 0), 6) if group else x_tiles(wide_at(9, 0), 8), "z_line%d" % group)
         for yo in (2, 1, 3):
             there = (NY - yo) % NY
             send(line, line_of(0, there, group), "y_line%d%d" % (there, group), at(yo, 0, 0))
         send(line, line_of(1, 0, group), "core", at(0, 0, 1))
-    arrived(x_tiles(8, (CLOSE - 1) * 8), "z_close")
+    pl.when(c == 1)(close_forward)
+    arrived(x_tiles(8, (CLOSE - 1) * 6), "z_close")
     send(x_tiles(0, CLOSE * 8), x_tiles(128, CLOSE * 8), "core", at(0, 0, 1))
 
     def halves(v):

time: 47.4 us -> 46.2 us (0.975)
  Pallas kernels: 45.6 us -> 44.3 us
    pallas_call x1, Pallas kernels: 45.6 us -> 44.3 us  [per_device(): pl.pallas_call(kernel, out_shape=jax.ShapeDtypeStruct((16, 256), F32), in...]
where the time goes in v4:
time: 46.2 us; the launch traced here: 45.6 us
  Pallas kernels  44.3 us (96%)
  local copies, waits for them, and re-layouts  1.32 us (3%)
    pallas_call x1, Pallas kernels, per_device(): pl.pallas_call(kernel, out_shape=jax.ShapeDtypeStruct((16, 256), F32), in...  44.3 us
    unnamed x1, local copies, waits for them, and re-layouts  1.32 us

profile of v4, /device:TPU:6, one launch (start us, length us, event | category | flops | bytes accessed | tf_op | source)
XLA Modules:
  0.0 45.6 jit_solution(15942779615122264198)
XLA Ops:
  0.0 44.3 %near_far_operator.1 = f32[16,256]{1,0:T(8,128)} custom-call(bf16[16,256]{1,0:T(8,128)(2,1)} %coeffs.1, bf16[40,128,128]{2,1,0:T(8,128)(2,1)} %blocks.1, s32[40]{0:T(128)} %scale.1, s32[40,128]{1,0:T(8,128)} %bitcast.2, s32[5120]{0:T(1024)} %nsrc.1, bf16[2,32,128]{2,1,0:T(8,128)(2,1)} %src_basis.1, bf16[2,32,128]{2,1,0:T(8,128)(2,1)} %tgt_basis.1, ...), custom_call_target="tpu_custom_call" | custom-call | flops 1000000000 | bytes 2000000 | tf_op jit(solution)/shard_map/near_far_operator/pallas_call | solution.py:390
  44.3 1.3 %copy.12 = f32[16,256]{1,0:T(8,128)} copy(f32[16,256]{1,0:T(8,128)} %near_far_operator.1) | data formatting | bytes 32768

commit v5 on v4

--- a/solution.py
+++ b/solution.py
@@ -14,8 +14,8 @@
 PAIRS = 32
 SHARE = 8
 SPLITS = (0, 16, 32, BLK)
-CLOSE = 7
-LINES = ((CLOSE, 13 - CLOSE), (13, 3))
+CLOSE = 3
+LINES = ((CLOSE, 9 - CLOSE), (9, 7))
 Z_ORDER = (8, 7, 9, 6, 10, 5, 11, 4, 12, 3, 13, 2, 14, 1, 15)
 TO_Z = Z_ORDER + (0,)
 FAR_AFTER = 1
@@ -23,12 +23,12 @@
 PARTS = 8
 PLACE = (0, 1, 3, 2)
 RECV_NAMES = (
-    "y_own", "z_own", "z_close", "z_line0", "z_line1", "y_line10", "y_line20", "y_line30", "y_line11", "y_line21", "y_line31", "core", "coup", "far", "f_swap", "pair",
+    "y_own", "z_own", "z_close", "z_line", "y_line10", "y_line20", "y_line30", "y_line11", "y_line21", "y_line31", "core", "coup", "far", "f_swap", "pair",
     "dense0", "dense1", "dense2", "dense3", "dense4", "dense5", "dense6", "dense7",
     "z_far", "z_near0", "z_near1", "z_near2", "z_near3",
 )
 RECV = {name: i for i, name in enumerate(RECV_NAMES)}
-SEND = dict(zip(RECV_NAMES, (0, 0, 0, 0, 0, 0, 0, 0, 0, 0, 0, 0, 1, 2, 3, 4, 5, 5, 5, 5, 5, 5, 5, 5, 6, 7, 7, 7, 7)))
+SEND = dict(zip(RECV_NAMES, (0, 0, 0, 0, 0, 0, 0, 0, 0, 0, 0, 1, 2, 3, 4, 5, 5, 5, 5, 5, 5, 5, 5, 6, 7, 7, 7, 7)))
 F32, BF16 = jnp.float32, jnp.bfloat16
 NT = (((1,), (1,)), ((), ()))
 
@@ -198,7 +198,16 @@
     arrived(x_tiles(8, 16), "z_own")
     for zo in (4, 3, 13, 2, 14, 1, 15):
         far = zo + 4 if zo < MID else zo - 4
-        send(piece(zo), piece(far), "z_line%d" % (NEAR.index(far) >= 13), at(0, zo - far, 0))
+        send(piece(zo), piece(far), "z_line", at(0, zo - far, 0))
+    def line_out(group):
+        line = line_of(0, 0, group)
+        for yo in (2, 1, 3):
+            there = (NY - yo) % NY
+            send(line, line_of(0, there, group), "y_line%d%d" % (there, group), at(yo, 0, 0))
+        send(line, line_of(1, 0, group), "core", at(0, 0, 1))
+
+    line_out(0)
+
     def close_forward():
         arrived(x_tiles(2, 6), "y_own")
         for zo in Z_ORDER[16 - CLOSE :]:
@@ -245,13 +254,8 @@
         return carry
 
     lax.fori_loop(0, BLK, find, 0)
-    for group in range(2):
-        line = line_of(0, 0, group)
-        arrived(x_tiles(wide_at(13, 0), 6) if group else x_tiles(wide_at(9, 0), 8), "z_line%d" % group)
-        for yo in (2, 1, 3):
-            there = (NY - yo) % NY
-            send(line, line_of(0, there, group), "y_line%d%d" % (there, group), at(yo, 0, 0))
-        send(line, line_of(1, 0, group), "core", at(0, 0, 1))
+    arrived(x_tiles(wide_at(9, 0), 14), "z_line")
+    line_out(1)
     pl.when(c == 1)(close_forward)
     arrived(x_tiles(8, (CLOSE - 1) * 6), "z_close")
     send(x_tiles(0, CLOSE * 8), x_tiles(128, CLOSE * 8), "core", at(0, 0, 1))

time: 46.2 us -> 45.5 us (0.985)
  no operation moved by 1% of the time
where the time goes in v5:
time: 45.5 us; the launch traced here: 45.3 us
  Pallas kernels  44 us (97%)
  local copies, waits for them, and re-layouts  1.32 us (3%)
    pallas_call x1, Pallas kernels, per_device(): pl.pallas_call(kernel, out_shape=jax.ShapeDtypeStruct((16, 256), F32), in...  44 us
    unnamed x1, local copies, waits for them, and re-layouts  1.32 us

profile of v5, /device:TPU:6, one launch (start us, length us, event | category | flops | bytes accessed | tf_op | source)
XLA Modules:
  0.0 45.3 jit_solution(2226871621273464420)
XLA Ops:
  0.0 44.0 %near_far_operator.1 = f32[16,256]{1,0:T(8,128)} custom-call(bf16[16,256]{1,0:T(8,128)(2,1)} %coeffs.1, bf16[40,128,128]{2,1,0:T(8,128)(2,1)} %blocks.1, s32[40]{0:T(128)} %scale.1, s32[40,128]{1,0:T(8,128)} %bitcast.2, s32[5120]{0:T(1024)} %nsrc.1, bf16[2,32,128]{2,1,0:T(8,128)(2,1)} %src_basis.1, bf16[2,32,128]{2,1,0:T(8,128)(2,1)} %tgt_basis.1, ...), custom_call_target="tpu_custom_call" | custom-call | flops 1000000000 | bytes 2000000 | tf_op jit(solution)/shard_map/near_far_operator/pallas_call | solution.py:394
  44.0 1.3 %copy.12 = f32[16,256]{1,0:T(8,128)} copy(f32[16,256]{1,0:T(8,128)} %near_far_operator.1) | data formatting | bytes 32768

commit v6 on v5

--- a/solution.py
+++ b/solution.py
@@ -106,14 +106,15 @@
     pl.semaphore_wait(barrier, 15)
 
     own = x_tiles(0, 2)
-    for yo in (2, 1, 3):
-        send(own, x_tiles(close_at(0, (NY - yo) % NY), 2), "y_own", at(yo, 0, 0))
     def piece(zo):
         slot = NEAR.index(zo % NZ)
         return x_tiles(close_at(slot, 0) if slot < CLOSE else wide_at(slot, 0), 2)
 
     for zo in DIRECT:
         send(own, piece(-zo), "z_own", at(0, zo, 0))
+
+    for yo in (2, 1, 3):
+        send(own, x_tiles(close_at(0, (NY - yo) % NY), 2), "y_own", at(yo, 0, 0))
 
     local[0].wait()
     i32 = lax.broadcasted_iota(jnp.int32, (32, 128), 0)

time: 45.5 us -> 45.5 us (level)
  no operation moved by 1% of the time
where the time goes in v6:
time: 45.5 us; the launch traced here: 45.3 us
  Pallas kernels  43.9 us (96%)
  local copies, waits for them, and re-layouts  1.32 us (3%)
    pallas_call x1, Pallas kernels, per_device(): pl.pallas_call(kernel, out_shape=jax.ShapeDtypeStruct((16, 256), F32), in...  43.9 us
    unnamed x1, local copies, waits for them, and re-layouts  1.32 us

profile of v6, /device:TPU:6, one launch (start us, length us, event | category | flops | bytes accessed | tf_op | source)
XLA Modules:
  0.0 45.3 jit_solution(15754885256393428532)
XLA Ops:
  0.0 43.9 %near_far_operator.1 = f32[16,256]{1,0:T(8,128)} custom-call(bf16[16,256]{1,0:T(8,128)(2,1)} %coeffs.1, bf16[40,128,128]{2,1,0:T(8,128)(2,1)} %blocks.1, s32[40]{0:T(128)} %scale.1, s32[40,128]{1,0:T(8,128)} %bitcast.2, s32[5120]{0:T(1024)} %nsrc.1, bf16[2,32,128]{2,1,0:T(8,128)(2,1)} %src_basis.1, bf16[2,32,128]{2,1,0:T(8,128)(2,1)} %tgt_basis.1, ...), custom_call_target="tpu_custom_call" | custom-call | flops 1000000000 | bytes 2000000 | tf_op jit(solution)/shard_map/near_far_operator/pallas_call | solution.py:395
  44.0 1.3 %copy.12 = f32[16,256]{1,0:T(8,128)} copy(f32[16,256]{1,0:T(8,128)} %near_far_operator.1) | data formatting | bytes 32768
